TPU v7x, 512 devices: a whole 4x4x16 slice. The times are simulated.
512 devices in a mesh: scan: 16 (over x, y_hi, core), depth: 32 (over z, y_lo).
Axes of the slice: x: 4, y: 4 (y_hi: 2, y_lo: 2; y = y_hi * 2 + y_lo), z: 16, core: 2. Of those that a mesh axis runs over, the one named last changes fastest.
Arguments:
- phase: float32 [32, 384, 384], P('depth'), may hold values from -3.140625 to 3.140625
- absorb: float32 [32, 384, 384], P('depth'), may hold values from 0 to 0.1
- probe: float32 [2, 128, 128], replicated, may hold values from -6 to 6
- offsets: int32 [128, 2], P('scan'), may hold values from 0 to 256
- measured: float32 [128, 128, 128], P('scan'), may hold values from 0 to 2
Outputs:
- grad_phase: float32 [32, 384, 384], P('depth', 'scan')
- grad_absorb: float32 [32, 384, 384], P('depth', 'scan')
All inputs are finite; a program needn't handle non-finite values.
Results may differ from a plain program's by a relative error of at most 0.0003.
Values sent between devices are 32-bit elements; how exact they have to be, the bound alone decides.
A program may use at most 64 MiB of HBM per device.

v0:
```python
import math

import jax
import jax.numpy as jnp
from jax import lax
from jax.sharding import PartitionSpec as P

chirp_rate = 1.0
highest = lax.Precision.HIGHEST


def shifted(block, axis, distance):
    devices = range(lax.axis_size(axis))
    route = [(i - distance, i) for i in devices if i - distance in devices]
    return lax.ppermute(block, axis, route)


def dft_table(win_size, sign):
    indices = jnp.arange(win_size, dtype=jnp.int32)
    products = indices[:, None] * indices[None, :] % win_size
    angles = 2.0 * math.pi / win_size * products.astype(jnp.float32)
    norm_scale = 1.0 / math.sqrt(win_size)
    real_part = jnp.cos(angles) * norm_scale
    imag_part = sign * jnp.sin(angles) * norm_scale
    return jnp.stack([jnp.stack([real_part, imag_part]), jnp.stack([-imag_part, real_part])])


def propagator(win_size):
    indices = jnp.arange(win_size, dtype=jnp.int32)
    signed = jnp.where(indices < win_size // 2, indices, indices - win_size).astype(jnp.float32)
    radius = signed[:, None] ** 2 + signed[None, :] ** 2
    angles = -chirp_rate * radius / win_size
    return jnp.stack([jnp.cos(angles), jnp.sin(angles)])


def complex_mul(first, second):
    return jnp.stack(
        [first[0] * second[0] - first[1] * second[1], first[0] * second[1] + first[1] * second[0]]
    )


def complex_conj(values):
    return jnp.stack([values[0], -values[1]])


def transform(values, table):
    half_done = jnp.einsum("cij,cdjk->dik", values, table, precision=highest)
    return jnp.einsum("cdij,cjk->dik", table, half_done, precision=highest)


def shards(phase, absorb, probe, offsets, measured):
    win_size = probe.shape[-1]
    num_pos = offsets.shape[0]
    sections = lax.axis_size("depth")
    section_idx = lax.axis_index("depth")
    is_last = section_idx == sections - 1
    is_first = section_idx == 0
    fwd_table = dft_table(win_size, -1.0)
    inv_table = dft_table(win_size, 1.0)
    prop_filt = propagator(win_size)
    back_filt = complex_conj(prop_filt)
    phase_local = phase[0]
    absorb_local = absorb[0]
    zero_wave = jnp.zeros((2, win_size, win_size), jnp.float32)

    def propagate(values, filt_table):
        return transform(complex_mul(filt_table, transform(values, fwd_table)), inv_table)

    def window_trans(slot_idx):
        row_off = offsets[slot_idx, 0]
        col_off = offsets[slot_idx, 1]
        phase_win = lax.dynamic_slice(phase_local, (row_off, col_off), (win_size, win_size))
        absorb_win = lax.dynamic_slice(absorb_local, (row_off, col_off), (win_size, win_size))
        amplitude = jnp.exp(-absorb_win)
        return jnp.stack([amplitude * jnp.cos(phase_win), amplitude * jnp.sin(phase_win)])

    def forward_work(slot_idx, incoming, stored):
        exit_stack, trans_stack, start_stack = stored
        trans_win = window_trans(slot_idx)
        wave_in = jnp.where(is_first, probe, incoming)
        exit_wave = complex_mul(wave_in, trans_win)

        def far_end():
            far_field = transform(exit_wave, fwd_table)
            target = lax.dynamic_index_in_dim(measured, slot_idx, 0, keepdims=False)
            residual = far_field[0] ** 2 + far_field[1] ** 2 - target
            adjoint = transform(residual[None] * far_field, inv_table)
            return (lax.dynamic_update_index_in_dim(start_stack, adjoint, slot_idx, 0), zero_wave)

        def onward():
            return (start_stack, propagate(exit_wave, prop_filt))

        start_stack, outgoing = lax.cond(is_last, far_end, onward)
        exit_stack = lax.dynamic_update_index_in_dim(exit_stack, exit_wave, slot_idx, 0)
        trans_stack = lax.dynamic_update_index_in_dim(trans_stack, trans_win, slot_idx, 0)
        return ((exit_stack, trans_stack, start_stack), outgoing)

    def forward_tick(step_no, incoming, stored):
        slot_raw = step_no - section_idx
        valid = (slot_raw >= 0) & (slot_raw < num_pos)
        slot_idx = jnp.clip(slot_raw, 0, num_pos - 1)
        return lax.cond(
            valid, lambda: forward_work(slot_idx, incoming, stored), lambda: (stored, zero_wave)
        )

    def backward_work(slot_idx, incoming, stored, gradients):
        exit_stack, trans_stack, start_stack = stored
        started = lax.dynamic_index_in_dim(start_stack, slot_idx, 0, keepdims=False)
        adjoint = jnp.where(is_last, started, incoming)
        exit_wave = lax.dynamic_index_in_dim(exit_stack, slot_idx, 0, keepdims=False)
        trans_win = lax.dynamic_index_in_dim(trans_stack, slot_idx, 0, keepdims=False)
        prod_re = exit_wave[0] * adjoint[0] + exit_wave[1] * adjoint[1]
        prod_im = exit_wave[0] * adjoint[1] - exit_wave[1] * adjoint[0]
        row_off = offsets[slot_idx, 0]
        col_off = offsets[slot_idx, 1]
        start = (jnp.int32(0), row_off, col_off)
        grad_patch = lax.dynamic_slice(gradients, start, (2, win_size, win_size))
        gradients = lax.dynamic_update_slice(
            gradients, grad_patch + jnp.stack([prod_im, -prod_re]), start
        )
        outgoing = propagate(complex_mul(complex_conj(trans_win), adjoint), back_filt)
        return (gradients, outgoing)

    def backward_tick(step_no, incoming, stored, gradients):
        slot_raw = step_no - (sections - 1 - section_idx)
        valid = (slot_raw >= 0) & (slot_raw < num_pos)
        slot_idx = jnp.clip(slot_raw, 0, num_pos - 1)
        return lax.cond(
            valid,
            lambda: backward_work(slot_idx, incoming, stored, gradients),
            lambda: (gradients, zero_wave),
        )

    stack_zero = jnp.zeros((num_pos, 2, win_size, win_size), jnp.float32)
    stored_zero = (stack_zero, stack_zero, stack_zero)
    grads_zero = jnp.zeros((2, phase_local.shape[0], phase_local.shape[1]), jnp.float32)

    def forward_step(step_no, loop_state):
        incoming, stored = loop_state
        stored, outgoing = forward_tick(step_no, incoming, stored)
        incoming = shifted(outgoing, "depth", 1)
        return (incoming, stored)

    _, stored = lax.fori_loop(0, num_pos + sections - 1, forward_step, (zero_wave, stored_zero))

    def backward_step(step_no, loop_state):
        incoming, gradients = loop_state
        gradients, outgoing = backward_tick(step_no, incoming, stored, gradients)
        incoming = shifted(outgoing, "depth", -1)
        return (incoming, gradients)

    _, gradients = lax.fori_loop(0, num_pos + sections - 1, backward_step, (zero_wave, grads_zero))
    reduced = lax.psum_scatter(gradients, "scan", scatter_dimension=1, tiled=True)
    return (reduced[0][None], reduced[1][None])


def solution(mesh):
    in_specs = (
        P("depth", None, None),
        P("depth", None, None),
        P(),
        P("scan", None),
        P("scan", None, None),
    )
    out_specs = (P("depth", "scan", None), P("depth", "scan", None))
    return jax.shard_map(shards, mesh=mesh, in_specs=in_specs, out_specs=out_specs, check_vma=False)
```

profile of v0, /device:TPU:2, one launch (start us, length us, event | category | flops | bytes accessed | tf_op | source)
XLA Modules:
  0.0 1446.5 jit_solution(2677353542599985023)
XLA Ops:
  10.8 524.9 %while.45 = (s32[]{:T(128)}, f32[2,128,128]{2,1,0:T(8,128)S(1)}, f32[8,2,128,128]{3,2,1,0:T(8,128)}, f32[8,2,128,128]{3,2,1,0:T(8,128)}, f32[8,2,128,128]{2,3,1,...) while((s32[]{:T(128)}, f32[2,128,128]{2,1,0:T(8,128)S(1)}, ...), condition=%wide.region_5.6_spmd.clone.clone.clone, body=%wide.region_0.5_spmd.clone.clone.clone.sunk | while | flops 403095552 | bytes 6227633 | solution.py:144
  149.4 14.6 %collective-permute-start = (f32[2,128,128]{2,1,0:T(8,128)}, f32[2,128,128]{2,1,0:T(8,128)S(1)}, u32[]{:S(2)}, u32[]{:S(2)}) collective-permute-start(f32[2,128,128]{2,1,0:T(8,128)} %get-tuple-element.1410), channel_id=1, source_target_pairs={{0,1},{1,2},{2,3},{3,4},{4,5},{5,6},{6,7},{7,8},{8,9},{9,10},{10,1... | collective-permute-start | bytes 393224 | tf_op jit(solution)/shard_map/while/body/eval_jaxpr/ppermute | solution.py:15
  176.2 14.6 %collective-permute-start = (f32[2,128,128]{2,1,0:T(8,128)}, f32[2,128,128]{2,1,0:T(8,128)S(1)}, u32[]{:S(2)}, u32[]{:S(2)}) collective-permute-start(f32[2,128,128]{2,1,0:T(8,128)} %get-tuple-element.1410), channel_id=1, source_target_pairs={{0,1},{1,2},{2,3},{3,4},{4,5},{5,6},{6,7},{7,8},{8,9},{9,10},{10,1... | collective-permute-start | bytes 393224 | tf_op jit(solution)/shard_map/while/body/eval_jaxpr/ppermute | solution.py:15
  298.1 12.3 collective-permute-start
  326.2 14.1 collective-permute-start
  379.3 11.0 collective-permute-start
  426.7 10.5 collective-permute-start
  472.9 12.2 collective-permute-start
  497.4 10.4 collective-permute-start
  520.6 10.9 collective-permute-start
  536.1 820.8 %while.46 = (s32[]{:T(128)}, f32[2,128,128]{1,2,0:T(8,128)S(1)}, f32[2,384,384]{2,1,0:T(8,128)S(1)}, s32[]{:T(128)}, s32[8,2]{0,1:T(2,128)S(1)}, /*index=5*/f32[...) while((s32[]{:T(128)}, f32[2,128,128]{1,2,0:T(8,128)S(1)}, ...), condition=%wide.region_9.10_spmd.clone.clone.clone, body=%wide.region_6.9_spmd.clone.clone.clone.sunk | while | flops 403193856 | bytes 5047264 | solution.py:152
  545.0 13.0 collective-permute-done.1
  590.1 14.4 collective-permute-done.1
  617.4 11.4 collective-permute-done.1
  640.7 10.3 collective-permute-done.1
  662.6 10.2 collective-permute-done.1
  683.4 11.7 collective-permute-done.1
  706.4 12.6 collective-permute-done.1
  730.7 10.4 collective-permute-done.1
  754.1 10.2 collective-permute-done.1
  796.5 11.9 collective-permute-done.1
  857.0 11.4 collective-permute-done.1
  869.8 329.2 %collective-permute-done.1 = f32[2,128,128]{1,2,0:T(8,128)S(1)} collective-permute-done((f32[2,128,128]{1,2,0:T(8,128)S(1)}, f32[2,128,128]{1,2,0:T(8,128)S(1)}, u32[]{:S(2)}, u32[]{:S(2)}) %collective-permute-start.1) | collective-permute-done | bytes 131104 | tf_op jit(solution)/shard_map/while/body/eval_jaxpr/ppermute | solution.py:15
  1199.1 10.4 conditional.13
  1218.8 10.4 conditional.13
  1238.0 10.4 conditional.13
  1256.9 10.3 conditional.13
  1286.7 11.3 collective-permute-done.1
  1298.1 10.4 conditional.13
  1327.7 11.8 collective-permute-done.1
  1339.6 10.4 conditional.13
  1358.0 80.3 %reduce-scatter.2.cloned.1.call-done = f32[2,24,384]{2,1,0:T(8,128)} async-done(((f32[2,384,384]{2,1,0:T(8,128)}), f32[2,24,384]{2,1,0:T(8,128)}) %reduce-scatter.2.cloned.1.call-update) | async-done | bytes 73744 | tf_op jit(solution)/shard_map/reduce_scatter | solution.py:153
  (612 shorter events, 845.5 us)
Async XLA Ops:
  7.2 1431.1 %reduce-scatter.2.cloned.1.call-start = ((), (), s32[]{:S(2)}) async-start(), calls=%async_computation.1 | async-start | bytes 1253376 | tf_op jit(solution)/shard_map/reduce_scatter | solution.py:153
  149.4 17.4 %collective-permute-start = (f32[2,128,128]{2,1,0:T(8,128)}, f32[2,128,128]{2,1,0:T(8,128)S(1)}, u32[]{:S(2)}, u32[]{:S(2)}) collective-permute-start(f32[2,128,128]{2,1,0:T(8,128)} %get-tuple-element.1410), channel_id=1, source_target_pairs={{0,1},{1,2},{2,3},{3,4},{4,5},{5,6},{6,7},{7,8},{8,9},{9,10},{10,1... | collective-permute-start | bytes 393224 | tf_op jit(solution)/shard_map/while/body/eval_jaxpr/ppermute | solution.py:15
  176.2 17.4 %collective-permute-start = (f32[2,128,128]{2,1,0:T(8,128)}, f32[2,128,128]{2,1,0:T(8,128)S(1)}, u32[]{:S(2)}, u32[]{:S(2)}) collective-permute-start(f32[2,128,128]{2,1,0:T(8,128)} %get-tuple-element.1410), channel_id=1, source_target_pairs={{0,1},{1,2},{2,3},{3,4},{4,5},{5,6},{6,7},{7,8},{8,9},{9,10},{10,1... | collective-permute-start | bytes 393224 | tf_op jit(solution)/shard_map/while/body/eval_jaxpr/ppermute | solution.py:15
  203.7 12.8 collective-permute-start
  227.7 12.4 collective-permute-start
  251.4 11.4 collective-permute-start
  273.5 13.0 collective-permute-start
  298.1 15.1 %collective-permute-start = (f32[2,128,128]{2,1,0:T(8,128)}, f32[2,128,128]{2,1,0:T(8,128)S(1)}, u32[]{:S(2)}, u32[]{:S(2)}) collective-permute-start(f32[2,128,128]{2,1,0:T(8,128)} %get-tuple-element.1410), channel_id=1, source_target_pairs={{0,1},{1,2},{2,3},{3,4},{4,5},{5,6},{6,7},{7,8},{8,9},{9,10},{10,1... | collective-permute-start | bytes 393224 | tf_op jit(solution)/shard_map/while/body/eval_jaxpr/ppermute | solution.py:15
  326.2 18.2 %collective-permute-start = (f32[2,128,128]{2,1,0:T(8,128)}, f32[2,128,128]{2,1,0:T(8,128)S(1)}, u32[]{:S(2)}, u32[]{:S(2)}) collective-permute-start(f32[2,128,128]{2,1,0:T(8,128)} %get-tuple-element.1410), channel_id=1, source_target_pairs={{0,1},{1,2},{2,3},{3,4},{4,5},{5,6},{6,7},{7,8},{8,9},{9,10},{10,1... | collective-permute-start | bytes 393224 | tf_op jit(solution)/shard_map/while/body/eval_jaxpr/ppermute | solution.py:15
  355.3 12.9 collective-permute-start
  379.3 13.8 collective-permute-start
  403.8 12.2 collective-permute-start
  426.7 14.6 %collective-permute-start = (f32[2,128,128]{2,1,0:T(8,128)}, f32[2,128,128]{2,1,0:T(8,128)S(1)}, u32[]{:S(2)}, u32[]{:S(2)}) collective-permute-start(f32[2,128,128]{2,1,0:T(8,128)} %get-tuple-element.1410), channel_id=1, source_target_pairs={{0,1},{1,2},{2,3},{3,4},{4,5},{5,6},{6,7},{7,8},{8,9},{9,10},{10,1... | collective-permute-start | bytes 393224 | tf_op jit(solution)/shard_map/while/body/eval_jaxpr/ppermute | solution.py:15
  450.4 12.7 collective-permute-start
  472.9 15.2 %collective-permute-start = (f32[2,128,128]{2,1,0:T(8,128)}, f32[2,128,128]{2,1,0:T(8,128)S(1)}, u32[]{:S(2)}, u32[]{:S(2)}) collective-permute-start(f32[2,128,128]{2,1,0:T(8,128)} %get-tuple-element.1410), channel_id=1, source_target_pairs={{0,1},{1,2},{2,3},{3,4},{4,5},{5,6},{6,7},{7,8},{8,9},{9,10},{10,1... | collective-permute-start | bytes 393224 | tf_op jit(solution)/shard_map/while/body/eval_jaxpr/ppermute | solution.py:15
  497.4 14.6 %collective-permute-start = (f32[2,128,128]{2,1,0:T(8,128)}, f32[2,128,128]{2,1,0:T(8,128)S(1)}, u32[]{:S(2)}, u32[]{:S(2)}) collective-permute-start(f32[2,128,128]{2,1,0:T(8,128)} %get-tuple-element.1410), channel_id=1, source_target_pairs={{0,1},{1,2},{2,3},{3,4},{4,5},{5,6},{6,7},{7,8},{8,9},{9,10},{10,1... | collective-permute-start | bytes 393224 | tf_op jit(solution)/shard_map/while/body/eval_jaxpr/ppermute | solution.py:15
  520.6 15.1 %collective-permute-start = (f32[2,128,128]{2,1,0:T(8,128)}, f32[2,128,128]{2,1,0:T(8,128)S(1)}, u32[]{:S(2)}, u32[]{:S(2)}) collective-permute-start(f32[2,128,128]{2,1,0:T(8,128)} %get-tuple-element.1410), channel_id=1, source_target_pairs={{0,1},{1,2},{2,3},{3,4},{4,5},{5,6},{6,7},{7,8},{8,9},{9,10},{10,1... | collective-permute-start | bytes 393224 | tf_op jit(solution)/shard_map/while/body/eval_jaxpr/ppermute | solution.py:15
  543.7 14.3 collective-permute-start.1
  588.8 15.7 %collective-permute-start.1 = (f32[2,128,128]{1,2,0:T(8,128)S(1)}, f32[2,128,128]{1,2,0:T(8,128)S(1)}, u32[]{:S(2)}, u32[]{:S(2)}) collective-permute-start(f32[2,128,128]{1,2,0:T(8,128)S(1)} %get-tuple-element.1426), channel_id=1, source_target_pairs={{1,0},{2,1},{3,2},{4,3},{5,4},{6,5},{7,6},{8,7},{9,8},{10,9},{11,1... | collective-permute-start | bytes 393224 | tf_op jit(solution)/shard_map/while/body/eval_jaxpr/ppermute | solution.py:15
  616.0 12.7 collective-permute-start.1
  639.3 11.6 collective-permute-start.1
  661.3 11.5 collective-permute-start.1
  682.1 13.0 collective-permute-start.1
  705.1 13.9 collective-permute-start.1
  729.4 11.7 collective-permute-start.1
  741.3 11.4 collective-permute-start.1
  752.8 11.5 collective-permute-start.1
  795.2 13.2 collective-permute-start.1
  855.7 12.7 collective-permute-start.1
  868.5 330.5 %collective-permute-start.1 = (f32[2,128,128]{1,2,0:T(8,128)S(1)}, f32[2,128,128]{1,2,0:T(8,128)S(1)}, u32[]{:S(2)}, u32[]{:S(2)}) collective-permute-start(f32[2,128,128]{1,2,0:T(8,128)S(1)} %get-tuple-element.1426), channel_id=1, source_target_pairs={{1,0},{2,1},{3,2},{4,3},{5,4},{6,5},{7,6},{8,7},{9,8},{10,9},{11,1... | collective-permute-start | bytes 393224 | tf_op jit(solution)/shard_map/while/body/eval_jaxpr/ppermute | solution.py:15
  1285.4 12.6 collective-permute-start.1
  1326.4 13.1 collective-permute-start.1
  (51 other events, 418.6 us)
Sparse Core Ops, SparseCore 0:
  1358.1 80.1 reduce-scatter.1
where the time goes:
time: 1450 us
  waiting for transfers between devices  881 us (61%)
  starting transfers between devices  351 us (24%)
  local copies, waits for them, and re-layouts  68 us (5%)
  loops' own time  64 us (4%)
  other arithmetic  36.3 us (3%)
  matrix products  31.8 us (2%)
    ppermute x78, waiting for transfers between devices, shifted(): return lax.ppermute(block, axis, route)  801 us
    ppermute x78, starting transfers between devices, shifted(): return lax.ppermute(block, axis, route)  351 us
    reduce_scatter x1, waiting for transfers between devices, shards(): lax.psum_scatter(gradients, 'scan', scatter_dimension=1, tiled=True)  80.3 us
    another operation x39, loops' own time, forward_tick(): lax.cond(valid, lambda: forward_work(slot_idx, incoming, stored), lambda:...  30.6 us
    another operation x39, loops' own time, backward_tick(): lax.cond(valid, lambda: backward_work(slot_idx, incoming, stored, gradien...  30 us
  transfers between devices with their start and end apart: 79, of which 79 were waited for; matrix products, arithmetic and copies ran while one was open for 0% of the time, Pallas kernels for 0%

commit v1 on v0

v1 whole, which is shorter than its diff:
```python
import functools

import jax
import jax.numpy as jnp
import ml_dtypes
import numpy as np
from jax import lax
from jax.experimental import pallas as pl
from jax.experimental.pallas import tpu as pltpu
from jax.sharding import PartitionSpec as P

MESH = pl.DeviceIdType.MESH
BF16 = jnp.bfloat16
F32 = jnp.float32
STRIDE = 4


def tables(win):
    idx = np.arange(win)
    ang = 2.0 * np.pi * (np.outer(idx, idx) % win) / win
    fwd = np.exp(-1j * ang) / np.sqrt(win)
    signed = np.where(idx < win // 2, idx, idx - win).astype(np.float64)
    chirp = np.exp(-1j * signed**2 / win)
    prop = np.conj(fwd) @ (chirp[:, None] * fwd)
    prop = 0.5 * (prop + prop.T)
    out = []
    for mat in (prop, fwd):
        right = np.block([[mat.real, mat.imag], [-mat.imag, mat.real]])
        left = np.block([[mat.real, -mat.imag], [mat.imag, mat.real]])
        for block in (right, left):
            block = block.astype(np.float32)
            high = block.astype(ml_dtypes.bfloat16)
            low = (block - high.astype(np.float32)).astype(ml_dtypes.bfloat16)
            out += [high, low]
    return np.stack(out)


def split(values):
    high = values.astype(BF16)
    low = (values - high.astype(F32)).astype(BF16)
    return high, low


def sandwich(re, im, tab, right, left):
    win = re.shape[0]
    high, low = split(jnp.concatenate([re, im], axis=1))
    both = jnp.concatenate([high, low], axis=0)
    main = jnp.dot(both, tab[right], preferred_element_type=F32)
    half = main[:win] + main[win:] + jnp.dot(high, tab[right + 1], preferred_element_type=F32)
    high, low = split(jnp.concatenate([half[:, :win], half[:, win:]], axis=0))
    both = jnp.concatenate([high, low], axis=1)
    main = jnp.dot(tab[left], both, preferred_element_type=F32)
    done = main[:, :win] + main[:, win:] + jnp.dot(tab[left + 1], high, preferred_element_type=F32)
    return done[:win], done[win:]


def window_kernel(off_ref, phase_ref, absorb_ref, out_ref, field):
    win = out_ref.shape[-1]
    obj = phase_ref.shape[-1]
    amp = jnp.exp(-absorb_ref[0])
    phase = phase_ref[0]
    field[0, :obj] = amp * jnp.cos(phase)
    field[1, :obj] = amp * jnp.sin(phase)

    def one(i, carry):
        row, col = off_ref[i, 0], off_ref[i, 1]
        high = lax.div(row, 8)
        low = row - 8 * high
        for part in range(2):
            rows = field[part, pl.ds(pl.multiple_of(8 * high, 8), win + 8), :]
            cols = pltpu.roll(rows, lax.rem(obj - col, obj), 1)[:, :win]
            out_ref[i, part] = pltpu.roll(cols, lax.rem(win + 8 - low, win + 8), 0)[:win]
        return carry

    lax.fori_loop(0, out_ref.shape[0], one, 0)


def field_kernel(off_ref, got_ref, out_ref, field):
    win = got_ref.shape[-1]
    obj = out_ref.shape[-1]
    field[...] = jnp.zeros_like(field)

    def one(i, carry):
        row, col = off_ref[i, 0], off_ref[i, 1]
        high = lax.div(row, 8)
        low = row - 8 * high
        for part in range(2):
            tall = jnp.concatenate([got_ref[i, part], jnp.zeros((8, win), F32)], axis=0)
            tall = pltpu.roll(tall, low, 0)
            wide = jnp.concatenate([tall, jnp.zeros((win + 8, obj - win), F32)], axis=1)
            field[part, pl.ds(pl.multiple_of(8 * high, 8), win + 8), :] += pltpu.roll(wide, col, 1)
        return carry

    lax.fori_loop(0, got_ref.shape[0], one, 0)
    out_ref[...] = field[:, :obj]


def chain_kernel(
    sections, num_pos, tw_ref, probe_ref, meas_ref, tab_ref, got_ref,
    trans, exits, wave, win_send, win_recv, grad_send, grad_recv,
):
    scan = lax.axis_index("scan")
    me = lax.axis_index("depth")
    shift = 3 * lax.rem(scan, 2)
    slot = lax.div(me + 4 - shift, STRIDE) - 1
    active = lax.rem(me + 4 - shift, STRIDE) == 0

    def home(i):
        return STRIDE * i + shift

    barrier = pltpu.get_barrier_semaphore()

    @pl.when(active)
    def _():
        def greet(d, carry):
            @pl.when(d != me)
            def _():
                pl.semaphore_signal(barrier, inc=1, device_id=(scan, d), device_id_type=MESH)
            return carry
        lax.fori_loop(0, sections, greet, 0)
        pl.semaphore_wait(barrier, sections - 1)

    @pl.when(jnp.logical_not(active))
    def _():
        def greet(i, carry):
            pl.semaphore_signal(barrier, inc=1, device_id=(scan, home(i)), device_id_type=MESH)
            return carry
        lax.fori_loop(0, num_pos, greet, 0)
        pl.semaphore_wait(barrier, num_pos)

    def window_copy(i):
        return pltpu.make_async_remote_copy(
            src_ref=tw_ref.at[i], dst_ref=trans.at[me], send_sem=win_send.at[i], recv_sem=win_recv.at[me],
            device_id=(scan, home(i)), device_id_type=MESH)

    def send_window(i, carry):
        @pl.when(home(i) != me)
        def _():
            window_copy(i).start()

        @pl.when(home(i) == me)
        def _():
            pltpu.make_async_copy(tw_ref.at[i], trans.at[me], win_recv.at[me]).start()
        return carry

    lax.fori_loop(0, num_pos, send_window, 0)

    def grad_copy(k):
        return pltpu.make_async_remote_copy(
            src_ref=exits.at[k], dst_ref=got_ref.at[slot], send_sem=grad_send.at[k], recv_sem=grad_recv.at[slot],
            device_id=(scan, k), device_id_type=MESH)

    @pl.when(active)
    def _():
        wave[...] = probe_ref[...]

        def step_in(k):
            pltpu.make_async_copy(tw_ref.at[0], trans.at[k], win_recv.at[k]).wait()
            tr, ti = trans[k, 0], trans[k, 1]
            wr, wi = wave[0], wave[1]
            er = wr * tr - wi * ti
            ei = wr * ti + wi * tr
            exits[k, 0] = er
            exits[k, 1] = ei
            return er, ei

        def forward(k, carry):
            er, ei = step_in(k)
            wr, wi = sandwich(er, ei, tab_ref, 0, 2)
            wave[0] = wr
            wave[1] = wi
            return carry

        lax.fori_loop(0, sections - 1, forward, 0)
        er, ei = step_in(sections - 1)
        fr, fi = sandwich(er, ei, tab_ref, 4, 6)
        resid = fr * fr + fi * fi - meas_ref[slot]
        lr, li = sandwich(resid * fr, resid * fi, tab_ref, 6, 4)
        wave[0] = lr
        wave[1] = li

        def grads(k):
            er, ei = exits[k, 0], exits[k, 1]
            lr, li = wave[0], wave[1]
            exits[k, 0] = er * li - ei * lr
            exits[k, 1] = -(er * lr + ei * li)

            @pl.when(k != me)
            def _():
                grad_copy(k).start()

            @pl.when(k == me)
            def _():
                pltpu.make_async_copy(exits.at[k], got_ref.at[slot], grad_recv.at[slot]).start()
            return lr, li

        def backward(j, carry):
            k = sections - 1 - j
            lr, li = grads(k)
            tr, ti = trans[k, 0], trans[k, 1]
            wr, wi = sandwich(tr * lr + ti * li, tr * li - ti * lr, tab_ref, 2, 0)
            wave[0] = wr
            wave[1] = wi
            return carry

        lax.fori_loop(0, sections - 1, backward, 0)
        grads(0)

    def finish(i, carry):
        @pl.when(home(i) != me)
        def _():
            window_copy(i).wait_send()
        pltpu.make_async_copy(tw_ref.at[0], got_ref.at[i], grad_recv.at[i]).wait()
        return carry

    lax.fori_loop(0, num_pos, finish, 0)

    @pl.when(active)
    def _():
        def drain(k, carry):
            @pl.when(k != me)
            def _():
                grad_copy(k).wait_send()
            return carry
        lax.fori_loop(0, sections, drain, 0)


def shards(tab, phase, absorb, probe, offsets, measured):
    win = probe.shape[-1]
    obj = phase.shape[-1]
    num_pos = offsets.shape[0]
    sections = lax.axis_size("depth")
    vmem = pl.BlockSpec(memory_space=pltpu.VMEM)
    smem = pl.BlockSpec(memory_space=pltpu.SMEM)
    limit = 48 * 1024 * 1024
    windows = pl.pallas_call(
        window_kernel,
        out_shape=jax.ShapeDtypeStruct((num_pos, 2, win, win), F32),
        in_specs=[smem, vmem, vmem],
        out_specs=vmem,
        scratch_shapes=[pltpu.VMEM((2, obj + 8, obj), F32)],
        compiler_params=pltpu.CompilerParams(vmem_limit_bytes=limit),
    )(offsets, phase, absorb)
    got = pl.pallas_call(
        functools.partial(chain_kernel, sections, num_pos),
        out_shape=jax.ShapeDtypeStruct((num_pos, 2, win, win), F32),
        in_specs=[vmem] * 4,
        out_specs=vmem,
        scratch_shapes=[
            pltpu.VMEM((sections, 2, win, win), F32),
            pltpu.VMEM((sections, 2, win, win), F32),
            pltpu.VMEM((2, win, win), F32),
            pltpu.SemaphoreType.DMA((num_pos,)),
            pltpu.SemaphoreType.DMA((sections,)),
            pltpu.SemaphoreType.DMA((sections,)),
            pltpu.SemaphoreType.DMA((num_pos,)),
        ],
        compiler_params=pltpu.CompilerParams(
            collective_id=0, has_side_effects=True, vmem_limit_bytes=limit),
    )(windows, probe, measured, tab)
    fields = pl.pallas_call(
        field_kernel,
        out_shape=jax.ShapeDtypeStruct((2, obj, obj), F32),
        in_specs=[smem, vmem],
        out_specs=vmem,
        scratch_shapes=[pltpu.VMEM((2, obj + 8, obj), F32)],
        compiler_params=pltpu.CompilerParams(vmem_limit_bytes=limit),
    )(offsets, got)
    reduced = lax.psum_scatter(fields, "scan", scatter_dimension=1, tiled=True)
    return reduced[0][None], reduced[1][None]


def solution(mesh):
    tab = tables(128)
    in_specs = (
        P("depth", None, None),
        P("depth", None, None),
        P(),
        P("scan", None),
        P("scan", None, None),
    )
    out_specs = (P("depth", "scan", None), P("depth", "scan", None))

    def run(phase, absorb, probe, offsets, measured):
        body = functools.partial(shards, jnp.asarray(tab))
        return jax.shard_map(body, mesh=mesh, in_specs=in_specs, out_specs=out_specs, check_vma=False)(
            phase, absorb, probe, offsets, measured)

    return run
```

time: 1450 us -> 259 us (0.18)
  the two profiles are of different devices: /device:TPU:2 before, /device:TPU:33 now
where the time goes in v1:
time: 259 us; the launch traced here: 256 us
  Pallas kernels  151 us (58%)
  waiting for transfers between devices  87.1 us (34%)
  between operations  14.1 us (5%)
  local copies, waits for them, and re-layouts  4.39 us (2%)
    pallas_call x1, Pallas kernels, shards(): pl.pallas_call(functools.partial(chain_kernel, sections, num_pos), out_sh...  143 us
    reduce_scatter x1, waiting for transfers between devices, shards(): reduced = lax.psum_scatter(fields, 'scan', scatter_dimension=1, tiled=True)  87.1 us
  transfers between devices with their start and end apart: 1, of which 1 were waited for; matrix products, arithmetic and copies ran while one was open for 0% of the time, Pallas kernels for 0%

profile of v1, /device:TPU:33, one launch (start us, length us, event | category | flops | bytes accessed | tf_op | source)
XLA Modules:
  0.0 256.3 jit_solution(16912602420048558579)
XLA Ops:
  7.2 0.0 copy-start
  7.2 0.0 reduce-scatter.2.cloned.1.call-start
  7.2 0.8 copy.9.off_ref
  8.1 0.0 copy-start.1
  8.1 1.1 copy-done.1
  9.1 0.0 copy-start.2
  9.1 1.1 copy-done.2
  10.2 0.0 copy-start.3
  10.2 0.0 copy-start.4
  10.2 4.4 %shard_map.77.tw_ref = f32[8,2,128,128]{3,2,1,0:T(8,128)S(1)} custom-call(s32[8,2]{1,0:T(8,128)S(1)} %copy.9.off_ref, f32[1,384,384]{2,1,0:T(8,128)S(1)} %copy-done.1, f32[1,384,384]{2,1,0:T(8,128)S(1)} %copy-done.2), custom_call_target="tpu_custom_call" | custom-call | tf_op jit(solution)/shard_map/pallas_call | solution.py:236
  14.6 0.0 copy-done
  14.6 0.0 copy-done.3
  14.6 0.0 copy-done.4
  14.6 143.3 %shard_map.78.got_ref = f32[8,2,128,128]{3,2,1,0:T(8,128)S(1)} custom-call(f32[8,2,128,128]{3,2,1,0:T(8,128)S(1)} %shard_map.77.tw_ref, f32[2,128,128]{2,1,0:T(8,128)S(1)} %copy-done.4, f32[8,128,128]{2,1,0:T(8,128)S(1)} %copy-done.3, bf16[8,256,256]{2,1,0:T(8,128)(2,1)S(1)} %copy-done), custom_call_target="tpu_custom_call" | custom-call | tf_op jit(solution)/shard_map/pallas_call | solution.py:244
  158.0 2.9 %shard_map.79 = f32[2,384,384]{2,1,0:T(8,128)} custom-call(s32[8,2]{1,0:T(8,128)S(1)} %copy.9.off_ref, f32[8,2,128,128]{3,2,1,0:T(8,128)S(1)} %shard_map.78.got_ref), custom_call_target="tpu_custom_call" | custom-call | tf_op jit(solution)/shard_map/pallas_call | solution.py:261
  160.9 0.0 reduce-scatter.2.cloned.1.call-update
  161.0 87.1 %reduce-scatter.2.cloned.1.call-done = f32[2,24,384]{2,1,0:T(8,128)} async-done(((f32[2,384,384]{2,1,0:T(8,128)}), f32[2,24,384]{2,1,0:T(8,128)}) %reduce-scatter.2.cloned.1.call-update) | async-done | bytes 73744 | tf_op jit(solution)/shard_map/reduce_scatter | solution.py:269
  248.0 1.4 fusion
Async XLA Ops:
  7.2 7.4 %copy-start = (bf16[8,256,256]{2,1,0:T(8,128)(2,1)S(1)}, bf16[8,256,256]{2,1,0:T(8,128)(2,1)}, u32[]{:S(2)}) copy-start(bf16[8,256,256]{2,1,0:T(8,128)(2,1)} %constant.2.clone.tab_ref) | copy-start | bytes 3145732
  7.2 240.9 %reduce-scatter.2.cloned.1.call-start = ((), (), s32[]{:S(2)}) async-start(), calls=%async_computation.1 | async-start | bytes 1253376 | tf_op jit(solution)/shard_map/reduce_scatter | solution.py:269
  8.1 1.1 copy-start.1
  9.1 1.1 copy-start.2
  10.2 4.4 %copy-start.3 = (f32[8,128,128]{2,1,0:T(8,128)S(1)}, f32[8,128,128]{2,1,0:T(8,128)}, u32[]{:S(2)}) copy-start(f32[8,128,128]{2,1,0:T(8,128)} %meas_ref.1) | copy-start | bytes 1572868
  10.2 4.4 %copy-start.4 = (f32[2,128,128]{2,1,0:T(8,128)S(1)}, f32[2,128,128]{2,1,0:T(8,128)}, u32[]{:S(2)}) copy-start(f32[2,128,128]{2,1,0:T(8,128)} %probe_ref.1) | copy-start | bytes 393220
Sparse Core Ops, SparseCore 0:
  161.1 86.9 reduce-scatter.1

commit v2 on v1

--- a/solution.py
+++ b/solution.py
@@ -223,6 +223,57 @@
                 grad_copy(k).wait_send()
             return carry
         lax.fori_loop(0, sections, drain, 0)
+
+
+def sum_kernel(parts_ref, phase_ref, absorb_ref, got, own_sem, send_sem, recv_sem):
+    me = lax.axis_index("scan")
+    depth = lax.axis_index("depth")
+    groups, rows = got.shape[0], got.shape[2]
+    barrier = pltpu.get_barrier_semaphore()
+
+    def peer(step):
+        return lax.rem(me + step, groups)
+
+    def greet(step, carry):
+        pl.semaphore_signal(barrier, inc=1, device_id=(peer(step), depth), device_id_type=MESH)
+        return carry
+
+    lax.fori_loop(1, groups, greet, 0)
+    own = pltpu.make_async_copy(parts_ref.at[:, pl.ds(me * rows, rows), :], got.at[me], own_sem)
+    own.start()
+    pl.semaphore_wait(barrier, groups - 1)
+
+    def strip(step):
+        to = peer(step)
+        return pltpu.make_async_remote_copy(
+            src_ref=parts_ref.at[:, pl.ds(to * rows, rows), :], dst_ref=got.at[me],
+            send_sem=send_sem.at[step], recv_sem=recv_sem.at[me],
+            device_id=(to, depth), device_id_type=MESH)
+
+    def send(step, carry):
+        strip(step).start()
+        return carry
+
+    lax.fori_loop(1, groups, send, 0)
+    own.wait()
+
+    def arrive(step, carry):
+        one = peer(step)
+        pltpu.make_async_copy(got.at[one], got.at[one], recv_sem.at[one]).wait()
+        return carry
+
+    lax.fori_loop(1, groups, arrive, 0)
+    total = got[0]
+    for i in range(1, groups):
+        total = total + got[i]
+    phase_ref[0] = total[0]
+    absorb_ref[0] = total[1]
+
+    def drain(step, carry):
+        strip(step).wait_send()
+        return carry
+
+    lax.fori_loop(1, groups, drain, 0)
 
 
 def shards(tab, phase, absorb, probe, offsets, measured):
@@ -266,8 +317,22 @@
         scratch_shapes=[pltpu.VMEM((2, obj + 8, obj), F32)],
         compiler_params=pltpu.CompilerParams(vmem_limit_bytes=limit),
     )(offsets, got)
-    reduced = lax.psum_scatter(fields, "scan", scatter_dimension=1, tiled=True)
-    return reduced[0][None], reduced[1][None]
+    groups = lax.axis_size("scan")
+    rows = obj // groups
+    return pl.pallas_call(
+        sum_kernel,
+        out_shape=[jax.ShapeDtypeStruct((1, rows, obj), F32)] * 2,
+        in_specs=[vmem],
+        out_specs=[vmem, vmem],
+        scratch_shapes=[
+            pltpu.VMEM((groups, 2, rows, obj), F32),
+            pltpu.SemaphoreType.DMA,
+            pltpu.SemaphoreType.DMA((groups,)),
+            pltpu.SemaphoreType.DMA((groups,)),
+        ],
+        compiler_params=pltpu.CompilerParams(
+            collective_id=1, has_side_effects=True, vmem_limit_bytes=limit),
+    )(fields)
 
 
 def solution(mesh):

time: 259 us -> 187 us (0.72)
  the two profiles are of different devices: /device:TPU:33 before, /device:TPU:17 now
where the time goes in v2:
time: 187 us
  Pallas kernels  182 us (97%)
  local copies, waits for them, and re-layouts  4.22 us (2%)
    pallas_call x1, Pallas kernels, shards(): pl.pallas_call(functools.partial(chain_kernel, sections, num_pos), out_sh...  152 us
    pallas_call x1, Pallas kernels, shards(): pl.pallas_call(sum_kernel, out_shape=[jax.ShapeDtypeStruct((1, rows, obj)...  23.6 us
    pallas_call x1, Pallas kernels, shards(): pl.pallas_call(window_kernel, out_shape=jax.ShapeDtypeStruct((num_pos, 2,...  4.4 us
    unnamed x13, local copies, waits for them, and re-layouts  4.22 us

profile of v2, /device:TPU:17, one launch (start us, length us, event | category | flops | bytes accessed | tf_op | source)
XLA Modules:
  0.0 187.0 jit_solution(14510749200274438573)
XLA Ops:
  0.6 0.0 copy-start
  0.6 0.8 copy.9.off_ref
  1.5 0.0 copy-start.1
  1.5 1.1 copy-done.1
  2.5 0.0 copy-start.2
  2.6 1.1 copy-done.2
  3.6 0.0 copy-start.3
  3.6 0.0 copy-start.4
  3.6 4.4 %shard_map.77.tw_ref = f32[8,2,128,128]{3,2,1,0:T(8,128)S(1)} custom-call(s32[8,2]{1,0:T(8,128)S(1)} %copy.9.off_ref, f32[1,384,384]{2,1,0:T(8,128)S(1)} %copy-done.1, f32[1,384,384]{2,1,0:T(8,128)S(1)} %copy-done.2), custom_call_target="tpu_custom_call" | custom-call | tf_op jit(solution)/shard_map/pallas_call | solution.py:287
  8.0 0.0 copy-done
  8.0 0.0 copy-done.3
  8.0 0.0 copy-done.4
  8.1 152.3 %shard_map.78.got_ref = f32[8,2,128,128]{3,2,1,0:T(8,128)S(1)} custom-call(f32[8,2,128,128]{3,2,1,0:T(8,128)S(1)} %shard_map.77.tw_ref, f32[2,128,128]{2,1,0:T(8,128)S(1)} %copy-done.4, f32[8,128,128]{2,1,0:T(8,128)S(1)} %copy-done.3, bf16[8,256,256]{2,1,0:T(8,128)(2,1)S(1)} %copy-done), custom_call_target="tpu_custom_call" | custom-call | tf_op jit(solution)/shard_map/pallas_call | solution.py:295
  160.3 1.9 %shard_map.79.parts_ref = f32[2,384,384]{2,1,0:T(8,128)S(1)} custom-call(s32[8,2]{1,0:T(8,128)S(1)} %copy.9.off_ref, f32[8,2,128,128]{3,2,1,0:T(8,128)S(1)} %shard_map.78.got_ref), custom_call_target="tpu_custom_call" | custom-call | tf_op jit(solution)/shard_map/pallas_call | solution.py:312
  162.3 23.6 %shard_map.80 = (f32[1,24,384]{2,1,0:T(8,128)S(1)}, f32[1,24,384]{2,1,0:T(8,128)S(1)}) custom-call(f32[2,384,384]{2,1,0:T(8,128)S(1)} %shard_map.79.parts_ref), custom_call_target="tpu_custom_call" | custom-call | tf_op jit(solution)/shard_map/pallas_call | solution.py:322
  185.8 0.6 copy.12
  186.4 0.6 copy.13
Async XLA Ops:
  0.6 7.4 %copy-start = (bf16[8,256,256]{2,1,0:T(8,128)(2,1)S(1)}, bf16[8,256,256]{2,1,0:T(8,128)(2,1)}, u32[]{:S(2)}) copy-start(bf16[8,256,256]{2,1,0:T(8,128)(2,1)} %constant.2.clone.tab_ref) | copy-start | bytes 3145732
  1.5 1.1 copy-start.1
  2.5 1.1 copy-start.2
  3.6 4.4 %copy-start.3 = (f32[8,128,128]{2,1,0:T(8,128)S(1)}, f32[8,128,128]{2,1,0:T(8,128)}, u32[]{:S(2)}) copy-start(f32[8,128,128]{2,1,0:T(8,128)} %meas_ref.1) | copy-start | bytes 1572868
  3.6 4.4 %copy-start.4 = (f32[2,128,128]{2,1,0:T(8,128)S(1)}, f32[2,128,128]{2,1,0:T(8,128)}, u32[]{:S(2)}) copy-start(f32[2,128,128]{2,1,0:T(8,128)} %probe_ref.1) | copy-start | bytes 393220

commit v3 on v1

--- a/solution.py
+++ b/solution.py
@@ -12,7 +12,9 @@
 MESH = pl.DeviceIdType.MESH
 BF16 = jnp.bfloat16
 F32 = jnp.float32
-STRIDE = 4
+LANES = 2
+SIDE = 4
+AHEAD = 12
 
 
 def tables(win):
@@ -54,22 +56,162 @@
     return done[:win], done[win:]
 
 
-def window_kernel(off_ref, phase_ref, absorb_ref, out_ref, field):
+def turned(index):
+    first, last = lax.div(index, 8), lax.rem(index, 2)
+    return index + 7 * (last - first)
+
+
+def place():
+    depth = lax.axis_index("depth")
+    return lax.axis_index("scan"), lax.div(depth, LANES), lax.rem(depth, LANES)
+
+
+def home(j, z):
+    scan = 2 * j + lax.rem(z, 2)
+    return scan, LANES * z + lax.rem(lax.div(scan, SIDE), 2)
+
+
+def corner(off_ref, j):
+    z = lax.div(lax.axis_index("depth"), LANES)
+    scan = 2 * j + lax.rem(z, 2)
+    return off_ref[scan, 0], off_ref[scan, 1]
+
+
+def around(scan, z, lane, planes, distance):
+    return scan, LANES * lax.rem(z + planes + distance, planes) + lane
+
+
+def strip_rows(z, rows):
+    return pl.ds(pl.multiple_of(turned(z) * rows, 8), rows)
+
+
+def gather_kernel(
+    off_ref, phase_ref, absorb_ref, field_ref, corner_ref,
+    raw, made, line, raw_sem, turn_sem, line_send, line_recv, send_sem, recv_sem,
+):
+    scan, z, lane = place()
+    groups = lax.axis_size("scan")
+    planes = lax.axis_size("depth") // LANES
+    rows = made.shape[1]
+    rounds = planes // 4
+    loads = []
+    for part, ref in enumerate((phase_ref, absorb_ref)):
+        src = ref.at[0, pl.ds(pl.multiple_of(scan * rows, 8), rows), :]
+        loads.append(pltpu.make_async_copy(src, raw.at[part], raw_sem.at[part]))
+        loads[-1].start()
+    to = (turned(z), LANES * turned(scan) + lane)
+    stays = turned(z) == scan
+    near = (-2, -1, 1, 2)
+
+    barrier = pltpu.get_barrier_semaphore()
+    for distance in near:
+        pl.semaphore_signal(
+            barrier, inc=1, device_id=around(scan, z, lane, planes, distance), device_id_type=MESH)
+
+    @pl.when(jnp.logical_not(stays))
+    def _():
+        pl.semaphore_signal(barrier, inc=1, device_id=to, device_id_type=MESH)
+
+    def greet(step, carry):
+        other = (lax.rem(scan + step, groups), LANES * z + lane)
+        pl.semaphore_signal(barrier, inc=1, device_id=other, device_id_type=MESH)
+        return carry
+
+    lax.fori_loop(1, groups, greet, 0)
+    line[...] = jnp.zeros_like(line)
+    line[:, : off_ref.shape[1]] = off_ref[...]
+    for load in loads:
+        load.wait()
+    amp = jnp.exp(-raw[1])
+    made[0] = amp * jnp.cos(raw[0])
+    made[1] = amp * jnp.sin(raw[0])
+
+    turn = pltpu.make_async_remote_copy(
+        src_ref=made, dst_ref=field_ref.at[:, strip_rows(turned(scan), rows), :],
+        send_sem=turn_sem.at[0], recv_sem=turn_sem.at[1], device_id=to, device_id_type=MESH)
+    stay = pltpu.make_async_copy(made, field_ref.at[:, strip_rows(z, rows), :], turn_sem.at[1])
+
+    @pl.when(stays)
+    def _():
+        pl.semaphore_wait(barrier, len(near) + groups - 1)
+        stay.start()
+
+    @pl.when(jnp.logical_not(stays))
+    def _():
+        pl.semaphore_wait(barrier, len(near) + groups)
+        turn.start()
+
+    own_line = line.at[pl.ds(lax.div(z, 2), 1), :]
+    own = pltpu.make_async_copy(own_line, corner_ref.at[pl.ds(scan, 1), :], line_recv.at[scan])
+    own.start()
+
+    def tell(step):
+        return pltpu.make_async_remote_copy(
+            src_ref=own_line, dst_ref=corner_ref.at[pl.ds(scan, 1), :],
+            send_sem=line_send.at[step], recv_sem=line_recv.at[scan],
+            device_id=(lax.rem(scan + step, groups), LANES * z + lane), device_id_type=MESH)
+
+    def start_tell(step, carry):
+        tell(step).start()
+        return carry
+
+    lax.fori_loop(1, groups, start_tell, 0)
+    stay.wait()
+
+    def passing(step, way, distance):
+        sign = 1 if way == 0 else -1
+        whose = lax.rem(z + planes - sign * 2 * step, planes)
+        block = field_ref.at[:, strip_rows(whose, rows), :]
+        return pltpu.make_async_remote_copy(
+            src_ref=block, dst_ref=block,
+            send_sem=send_sem.at[way, step, distance - 1], recv_sem=recv_sem.at[way, step, distance - 1],
+            device_id=around(scan, z, lane, planes, sign * distance), device_id_type=MESH)
+
+    def goes(step, way, distance):
+        return not (way == 1 and step == rounds - 1 and distance == 2)
+
+    plan = [(step, way, distance) for step in range(rounds) for distance in (2, 1) for way in range(2)
+            if goes(step, way, distance)]
+    for step, way, distance in plan:
+        if step > 0 and (distance == 2 or not goes(step, way, 2)):
+            passing(step - 1, way, 2).wait_recv()
+        passing(step, way, distance).start()
+    passing(rounds - 1, 0, 2).wait_recv()
+    for step, way, distance in plan:
+        if distance == 1:
+            passing(step, way, distance).wait_recv()
+    for step, way, distance in plan:
+        passing(step, way, distance).wait_send()
+
+    @pl.when(jnp.logical_not(stays))
+    def _():
+        turn.wait_send()
+
+    def end_tell(step, carry):
+        one = lax.rem(scan + step, groups)
+        pltpu.make_async_copy(own_line, corner_ref.at[pl.ds(one, 1), :], line_recv.at[one]).wait()
+
+        @pl.when(step > 0)
+        def _():
+            tell(step).wait_send()
+        return carry
+
+    lax.fori_loop(0, groups, end_tell, 0)
+
+
+def window_kernel(off_ref, field_ref, out_ref, field):
     win = out_ref.shape[-1]
-    obj = phase_ref.shape[-1]
-    amp = jnp.exp(-absorb_ref[0])
-    phase = phase_ref[0]
-    field[0, :obj] = amp * jnp.cos(phase)
-    field[1, :obj] = amp * jnp.sin(phase)
-
-    def one(i, carry):
-        row, col = off_ref[i, 0], off_ref[i, 1]
+    obj = field_ref.shape[-1]
+    field[:, :obj] = field_ref[...]
+
+    def one(j, carry):
+        row, col = corner(off_ref, j)
         high = lax.div(row, 8)
         low = row - 8 * high
         for part in range(2):
             rows = field[part, pl.ds(pl.multiple_of(8 * high, 8), win + 8), :]
             cols = pltpu.roll(rows, lax.rem(obj - col, obj), 1)[:, :win]
-            out_ref[i, part] = pltpu.roll(cols, lax.rem(win + 8 - low, win + 8), 0)[:win]
+            out_ref[j, part] = pltpu.roll(cols, lax.rem(win + 8 - low, win + 8), 0)[:win]
         return carry
 
     lax.fori_loop(0, out_ref.shape[0], one, 0)
@@ -80,12 +222,12 @@
     obj = out_ref.shape[-1]
     field[...] = jnp.zeros_like(field)
 
-    def one(i, carry):
-        row, col = off_ref[i, 0], off_ref[i, 1]
+    def one(j, carry):
+        row, col = corner(off_ref, j)
         high = lax.div(row, 8)
         low = row - 8 * high
         for part in range(2):
-            tall = jnp.concatenate([got_ref[i, part], jnp.zeros((8, win), F32)], axis=0)
+            tall = jnp.concatenate([got_ref[j, part], jnp.zeros((8, win), F32)], axis=0)
             tall = pltpu.roll(tall, low, 0)
             wide = jnp.concatenate([tall, jnp.zeros((win + 8, obj - win), F32)], axis=1)
             field[part, pl.ds(pl.multiple_of(8 * high, 8), win + 8), :] += pltpu.roll(wide, col, 1)
@@ -97,58 +239,93 @@
 
 def chain_kernel(
     sections, num_pos, tw_ref, probe_ref, meas_ref, tab_ref, got_ref,
-    trans, exits, wave, win_send, win_recv, grad_send, grad_recv,
+    trans, exits, wave, go_sem, win_send, win_recv, grad_send, grad_recv,
 ):
-    scan = lax.axis_index("scan")
-    me = lax.axis_index("depth")
-    shift = 3 * lax.rem(scan, 2)
-    slot = lax.div(me + 4 - shift, STRIDE) - 1
-    active = lax.rem(me + 4 - shift, STRIDE) == 0
-
-    def home(i):
-        return STRIDE * i + shift
+    scan, z, lane = place()
+    depth = LANES * z + lane
+    mine = 2 * turned(scan) + lane
+    slot = lax.div(z, 2)
+    member = lax.div(scan, 2)
+
+    def is_home(on_scan, on_lane):
+        return jnp.logical_and(lax.rem(on_scan, 2) == lax.rem(z, 2), on_lane == lax.rem(lax.div(on_scan, SIDE), 2))
+
+    active = is_home(scan, lane)
+
+    def owner(k):
+        return turned(lax.div(k, LANES)), LANES * z + lax.rem(k, LANES)
 
     barrier = pltpu.get_barrier_semaphore()
 
     @pl.when(active)
     def _():
-        def greet(d, carry):
-            @pl.when(d != me)
+        def greet(k, carry):
+            @pl.when(k != mine)
             def _():
-                pl.semaphore_signal(barrier, inc=1, device_id=(scan, d), device_id_type=MESH)
+                pl.semaphore_signal(barrier, inc=1, device_id=owner(k), device_id_type=MESH)
             return carry
         lax.fori_loop(0, sections, greet, 0)
         pl.semaphore_wait(barrier, sections - 1)
 
     @pl.when(jnp.logical_not(active))
     def _():
-        def greet(i, carry):
-            pl.semaphore_signal(barrier, inc=1, device_id=(scan, home(i)), device_id_type=MESH)
+        def greet(j, carry):
+            pl.semaphore_signal(barrier, inc=1, device_id=home(j, z), device_id_type=MESH)
             return carry
         lax.fori_loop(0, num_pos, greet, 0)
         pl.semaphore_wait(barrier, num_pos)
 
-    def window_copy(i):
+    def is_here(j):
+        return jnp.logical_and(active, j == member)
+
+    def window_copy(j):
         return pltpu.make_async_remote_copy(
-            src_ref=tw_ref.at[i], dst_ref=trans.at[me], send_sem=win_send.at[i], recv_sem=win_recv.at[me],
-            device_id=(scan, home(i)), device_id_type=MESH)
-
-    def send_window(i, carry):
-        @pl.when(home(i) != me)
+            src_ref=tw_ref.at[j], dst_ref=trans.at[mine], send_sem=win_send.at[j], recv_sem=win_recv.at[mine],
+            device_id=home(j, z), device_id_type=MESH)
+
+    def send_window(step, carry):
+        j = lax.rem(step + member, num_pos)
+        here = is_here(j)
+
+        @pl.when(jnp.logical_not(here))
         def _():
-            window_copy(i).start()
-
-        @pl.when(home(i) == me)
+            window_copy(j).start()
+
+        @pl.when(here)
         def _():
-            pltpu.make_async_copy(tw_ref.at[i], trans.at[me], win_recv.at[me]).start()
-        return carry
-
-    lax.fori_loop(0, num_pos, send_window, 0)
+            pltpu.make_async_copy(tw_ref.at[j], trans.at[mine], win_recv.at[mine]).start()
+        return carry
+
+    def send_windows():
+        lax.fori_loop(0, num_pos, send_window, 0)
+
+    @pl.when(mine < AHEAD)
+    def _():
+        send_windows()
+
+    @pl.when(jnp.logical_and(jnp.logical_not(active), mine >= AHEAD))
+    def _():
+        pl.semaphore_wait(go_sem, 1)
+        send_windows()
+
+    def call_up(k):
+        @pl.when(jnp.logical_and(k == mine, k >= AHEAD))
+        def _():
+            send_windows()
+
+        to, on_plane = owner(k)
+        on_lane = on_plane - LANES * z
+        awaits = jnp.logical_not(is_home(to, on_lane))
+        chosen = jnp.logical_and(lax.rem(k, num_pos) == member, k < sections)
+
+        @pl.when(jnp.logical_and(awaits, chosen))
+        def _():
+            pl.semaphore_signal(go_sem, inc=1, device_id=owner(k), device_id_type=MESH)
 
     def grad_copy(k):
         return pltpu.make_async_remote_copy(
-            src_ref=exits.at[k], dst_ref=got_ref.at[slot], send_sem=grad_send.at[k], recv_sem=grad_recv.at[slot],
-            device_id=(scan, k), device_id_type=MESH)
+            src_ref=exits.at[k], dst_ref=got_ref.at[member], send_sem=grad_send.at[k],
+            recv_sem=grad_recv.at[member], device_id=owner(k), device_id_type=MESH)
 
     @pl.when(active)
     def _():
@@ -165,6 +342,7 @@
             return er, ei
 
         def forward(k, carry):
+            call_up(k + AHEAD)
             er, ei = step_in(k)
             wr, wi = sandwich(er, ei, tab_ref, 0, 2)
             wave[0] = wr
@@ -185,13 +363,13 @@
             exits[k, 0] = er * li - ei * lr
             exits[k, 1] = -(er * lr + ei * li)
 
-            @pl.when(k != me)
+            @pl.when(k != mine)
             def _():
                 grad_copy(k).start()
 
-            @pl.when(k == me)
+            @pl.when(k == mine)
             def _():
-                pltpu.make_async_copy(exits.at[k], got_ref.at[slot], grad_recv.at[slot]).start()
+                pltpu.make_async_copy(exits.at[k], got_ref.at[member], grad_recv.at[member]).start()
             return lr, li
 
         def backward(j, carry):
@@ -206,11 +384,11 @@
         lax.fori_loop(0, sections - 1, backward, 0)
         grads(0)
 
-    def finish(i, carry):
-        @pl.when(home(i) != me)
+    def finish(j, carry):
+        @pl.when(jnp.logical_not(is_here(j)))
         def _():
-            window_copy(i).wait_send()
-        pltpu.make_async_copy(tw_ref.at[0], got_ref.at[i], grad_recv.at[i]).wait()
+            window_copy(j).wait_send()
+        pltpu.make_async_copy(tw_ref.at[0], got_ref.at[j], grad_recv.at[j]).wait()
         return carry
 
     lax.fori_loop(0, num_pos, finish, 0)
@@ -218,11 +396,95 @@
     @pl.when(active)
     def _():
         def drain(k, carry):
-            @pl.when(k != me)
+            @pl.when(k != mine)
             def _():
                 grad_copy(k).wait_send()
             return carry
         lax.fori_loop(0, sections, drain, 0)
+
+
+def sum_kernel(parts_ref, phase_ref, absorb_ref, got, made, last, turn_sem, send_sem, recv_sem):
+    scan, z, lane = place()
+    planes = lax.axis_size("depth") // LANES
+    rows = last.shape[2]
+    rounds = planes // 4
+    to = (turned(z), LANES * turned(scan) + lane)
+    stays = turned(z) == scan
+    near = (-2, -1, 1, 2)
+    barrier = pltpu.get_barrier_semaphore()
+    for distance in near:
+        pl.semaphore_signal(
+            barrier, inc=1, device_id=around(scan, z, lane, planes, distance), device_id_type=MESH)
+
+    @pl.when(jnp.logical_not(stays))
+    def _():
+        pl.semaphore_signal(barrier, inc=1, device_id=to, device_id_type=MESH)
+        pl.semaphore_wait(barrier, len(near) + 1)
+
+    @pl.when(stays)
+    def _():
+        pl.semaphore_wait(barrier, len(near))
+
+    def strip(way, ahead):
+        sign = 1 if way == 0 else -1
+        return parts_ref.at[:, strip_rows(lax.rem(z + planes + sign * ahead, planes), rows), :]
+
+    def goes(step, way, distance):
+        return not (way == 1 and step == 0 and distance == 2)
+
+    def passing(step, way, distance):
+        ahead = planes // 2 - 2 * step - (2 - distance)
+        bare = distance == 1 or step == 0 or (way == 1 and step == 0)
+        return pltpu.make_async_remote_copy(
+            src_ref=strip(way, ahead) if bare else made.at[way, step - 1],
+            dst_ref=got.at[way, step, distance - 1],
+            send_sem=send_sem.at[way, step, distance - 1], recv_sem=recv_sem.at[way, step, distance - 1],
+            device_id=around(scan, z, lane, planes, distance if way == 0 else -distance), device_id_type=MESH)
+
+    def arrived(step, way):
+        passing(step, way, 1).wait_recv()
+        total = got[way, step, 0]
+        if goes(step, way, 2):
+            passing(step, way, 2).wait_recv()
+            total = total + got[way, step, 1]
+        return total
+
+    for way in range(2):
+        if goes(0, way, 2):
+            passing(0, way, 2).start()
+    for way in range(2):
+        passing(0, way, 1).start()
+    for way in range(2):
+        passing(1, way, 1).start()
+    for step in range(1, rounds):
+        for way in range(2):
+            ahead = planes // 2 - 2 * step
+            made[way, step - 1] = strip(way, ahead)[...] + arrived(step - 1, way)
+            passing(step, way, 2).start()
+        if step + 1 < rounds:
+            for way in range(2):
+                passing(step + 1, way, 1).start()
+    last[0] = strip(0, 0)[...] + (arrived(rounds - 1, 0) + arrived(rounds - 1, 1))
+    turn = pltpu.make_async_remote_copy(
+        src_ref=last.at[0], dst_ref=last.at[1], send_sem=turn_sem.at[0], recv_sem=turn_sem.at[1],
+        device_id=to, device_id_type=MESH)
+
+    @pl.when(jnp.logical_not(stays))
+    def _():
+        turn.start()
+        turn.wait()
+
+    @pl.when(stays)
+    def _():
+        last[1] = last[0]
+
+    phase_ref[0] = last[1, 0]
+    absorb_ref[0] = last[1, 1]
+    for step in range(rounds):
+        for way in range(2):
+            for distance in (1, 2):
+                if goes(step, way, distance):
+                    passing(step, way, distance).wait_send()
 
 
 def shards(tab, phase, absorb, probe, offsets, measured):
@@ -232,15 +494,41 @@
     sections = lax.axis_size("depth")
     vmem = pl.BlockSpec(memory_space=pltpu.VMEM)
     smem = pl.BlockSpec(memory_space=pltpu.SMEM)
+    anywhere = pl.BlockSpec(memory_space=pl.ANY)
     limit = 48 * 1024 * 1024
+    groups = lax.axis_size("scan")
+    rows = obj // groups
+    rounds = sections // LANES // 4
+    field, corners = pl.pallas_call(
+        gather_kernel,
+        out_shape=[
+            jax.ShapeDtypeStruct((2, obj, obj), F32),
+            jax.ShapeDtypeStruct((groups, 128), jnp.int32),
+        ],
+        in_specs=[vmem, anywhere, anywhere],
+        out_specs=[vmem, vmem],
+        scratch_shapes=[
+            pltpu.VMEM((2, rows, obj), F32),
+            pltpu.VMEM((2, rows, obj), F32),
+            pltpu.VMEM((num_pos, 128), jnp.int32),
+            pltpu.SemaphoreType.DMA((2,)),
+            pltpu.SemaphoreType.DMA((2,)),
+            pltpu.SemaphoreType.DMA((groups,)),
+            pltpu.SemaphoreType.DMA((groups,)),
+            pltpu.SemaphoreType.DMA((2, rounds, 2)),
+            pltpu.SemaphoreType.DMA((2, rounds, 2)),
+        ],
+        compiler_params=pltpu.CompilerParams(
+            collective_id=2, has_side_effects=True, vmem_limit_bytes=60 * 1024 * 1024),
+    )(offsets, phase, absorb)
     windows = pl.pallas_call(
         window_kernel,
         out_shape=jax.ShapeDtypeStruct((num_pos, 2, win, win), F32),
-        in_specs=[smem, vmem, vmem],
+        in_specs=[smem, vmem],
         out_specs=vmem,
         scratch_shapes=[pltpu.VMEM((2, obj + 8, obj), F32)],
         compiler_params=pltpu.CompilerParams(vmem_limit_bytes=limit),
-    )(offsets, phase, absorb)
+    )(corners, field)
     got = pl.pallas_call(
         functools.partial(chain_kernel, sections, num_pos),
         out_shape=jax.ShapeDtypeStruct((num_pos, 2, win, win), F32),
@@ -250,6 +538,7 @@
             pltpu.VMEM((sections, 2, win, win), F32),
             pltpu.VMEM((sections, 2, win, win), F32),
             pltpu.VMEM((2, win, win), F32),
+            pltpu.SemaphoreType.REGULAR,
             pltpu.SemaphoreType.DMA((num_pos,)),
             pltpu.SemaphoreType.DMA((sections,)),
             pltpu.SemaphoreType.DMA((sections,)),
@@ -265,9 +554,23 @@
         out_specs=vmem,
         scratch_shapes=[pltpu.VMEM((2, obj + 8, obj), F32)],
         compiler_params=pltpu.CompilerParams(vmem_limit_bytes=limit),
-    )(offsets, got)
-    reduced = lax.psum_scatter(fields, "scan", scatter_dimension=1, tiled=True)
-    return reduced[0][None], reduced[1][None]
+    )(corners, got)
+    return pl.pallas_call(
+        sum_kernel,
+        out_shape=[jax.ShapeDtypeStruct((1, rows, obj), F32)] * 2,
+        in_specs=[vmem],
+        out_specs=[vmem, vmem],
+        scratch_shapes=[
+            pltpu.VMEM((2, rounds, 2, 2, rows, obj), F32),
+            pltpu.VMEM((2, rounds - 1, 2, rows, obj), F32),
+            pltpu.VMEM((2, 2, rows, obj), F32),
+            pltpu.SemaphoreType.DMA((2,)),
+            pltpu.SemaphoreType.DMA((2, rounds, 2)),
+            pltpu.SemaphoreType.DMA((2, rounds, 2)),
+        ],
+        compiler_params=pltpu.CompilerParams(
+            collective_id=1, has_side_effects=True, vmem_limit_bytes=limit),
+    )(fields)
 
 
 def solution(mesh):

time: 259 us -> 168 us (0.65)
  waiting for transfers between devices: 87.1 us -> 0 us
  between operations: 14.1 us -> 0.7 us
  Pallas kernels: 151 us -> 162 us
    pallas_call x0 -> x2, Pallas kernels: none -> 87.4 us  [the longest x1 45.1 us: shards(): pl.pallas_call(sum_kernel, out_shape=[jax.ShapeDtypeStruct((1, rows, obj)...]
    reduce_scatter x1 -> x0, waiting for transfers between devices: 87.1 us -> none  [shards(): reduced = lax.psum_scatter(fields, 'scan', scatter_dimension=1, tiled=True)]
    pallas_call x1, Pallas kernels: 143 us -> 70.3 us  [shards(): pl.pallas_call(functools.partial(chain_kernel, sections, num_pos), out_sh...]
  transfers between devices with their start and end apart: 1 -> 0, of which waited for: 1 -> 0; matrix products, arithmetic and copies ran while one was open for 0% -> 0% of each run, Pallas kernels for 0% -> 0%
where the time goes in v3:
time: 168 us
  Pallas kernels  162 us (96%)
  local copies, waits for them, and re-layouts  4.55 us (3%)
    pallas_call x1, Pallas kernels, shards(): pl.pallas_call(functools.partial(chain_kernel, sections, num_pos), out_sh...  70.3 us
    pallas_call x1, Pallas kernels, shards(): pl.pallas_call(sum_kernel, out_shape=[jax.ShapeDtypeStruct((1, rows, obj)...  45.1 us
    pallas_call x1, Pallas kernels, shards(): pl.pallas_call(gather_kernel, out_shape=[jax.ShapeDtypeStruct((2, obj, ob...  42.3 us
    unnamed x13, local copies, waits for them, and re-layouts  4.55 us

profile of v3, /device:TPU:33, one launch (start us, length us, event | category | flops | bytes accessed | tf_op | source)
XLA Modules:
  0.0 167.5 jit_solution(9904412757011391125)
XLA Ops:
  0.6 1.3 copy.8.off_ref
  2.0 0.0 copy-start.1
  2.0 0.0 copy-start.3
  2.0 42.3 %shard_map.77 = (f32[2,384,384]{2,1,0:T(8,128)}, s32[16,128]{1,0:T(8,128)}) custom-call(s32[8,2]{1,0:T(8,128)} %copy.8.off_ref, f32[1,384,384]{2,1,0:T(8,128)} %phase_ref.1, f32[1,384,384]{2,1,0:T(8,128)} %absorb_ref.1), custom_call_target="tpu_custom_call" | custom-call | tf_op jit(solution)/shard_map/pallas_call | solution.py:502
  44.3 0.0 copy-start
  44.3 1.3 copy-done
  45.6 0.0 copy-start.4
  45.6 0.7 copy-done.4
  46.3 0.0 copy-start.2
  46.3 2.5 %shard_map.78.tw_ref = f32[8,2,128,128]{3,2,1,0:T(8,128)S(1)} custom-call(s32[16,128]{1,0:T(8,128)S(1)} %copy-done.4, f32[2,384,384]{2,1,0:T(8,128)S(1)} %copy-done), custom_call_target="tpu_custom_call" | custom-call | tf_op jit(solution)/shard_map/pallas_call | solution.py:524
  48.7 0.0 copy-done.1
  48.8 0.0 copy-done.3
  48.8 0.0 copy-done.2
  48.8 70.3 %shard_map.79.got_ref = f32[8,2,128,128]{3,2,1,0:T(8,128)S(1)} custom-call(f32[8,2,128,128]{3,2,1,0:T(8,128)S(1)} %shard_map.78.tw_ref, f32[2,128,128]{2,1,0:T(8,128)S(1)} %copy-done.3, f32[8,128,128]{2,1,0:T(8,128)S(1)} %copy-done.2, bf16[8,256,256]{2,1,0:T(8,128)(2,1)S(1)} %copy-done.1), custom_call_target="tpu_custom_call" | custom-call | tf_op jit(solution)/shard_map/pallas_call | solution.py:532
  119.1 2.1 %shard_map.80.parts_ref = f32[2,384,384]{2,1,0:T(8,128)S(1)} custom-call(s32[16,128]{1,0:T(8,128)S(1)} %copy-done.4, f32[8,2,128,128]{3,2,1,0:T(8,128)S(1)} %shard_map.79.got_ref), custom_call_target="tpu_custom_call" | custom-call | tf_op jit(solution)/shard_map/pallas_call | solution.py:550
  121.2 45.1 %shard_map.81 = (f32[1,24,384]{2,1,0:T(8,128)S(1)}, f32[1,24,384]{2,1,0:T(8,128)S(1)}) custom-call(f32[2,384,384]{2,1,0:T(8,128)S(1)} %shard_map.80.parts_ref), custom_call_target="tpu_custom_call" | custom-call | tf_op jit(solution)/shard_map/pallas_call | solution.py:558
  166.3 0.6 copy.11
  166.9 0.6 copy.12
Async XLA Ops:
  2.0 46.8 %copy-start.1 = (bf16[8,256,256]{2,1,0:T(8,128)(2,1)S(1)}, bf16[8,256,256]{2,1,0:T(8,128)(2,1)}, u32[]{:S(2)}) copy-start(bf16[8,256,256]{2,1,0:T(8,128)(2,1)} %constant.2.clone.tab_ref) | copy-start | bytes 3145732
  2.0 46.8 %copy-start.3 = (f32[2,128,128]{2,1,0:T(8,128)S(1)}, f32[2,128,128]{2,1,0:T(8,128)}, u32[]{:S(2)}) copy-start(f32[2,128,128]{2,1,0:T(8,128)} %probe_ref.1) | copy-start | bytes 393220
  44.3 1.3 copy-start
  45.6 0.7 copy-start.4
  46.3 2.5 %copy-start.2 = (f32[8,128,128]{2,1,0:T(8,128)S(1)}, f32[8,128,128]{2,1,0:T(8,128)}, u32[]{:S(2)}) copy-start(f32[8,128,128]{2,1,0:T(8,128)} %meas_ref.1) | copy-start | bytes 1572868

commit v4 on v3

--- a/solution.py
+++ b/solution.py
@@ -14,7 +14,7 @@
 F32 = jnp.float32
 LANES = 2
 SIDE = 4
-AHEAD = 12
+AHEAD = 14
 
 
 def tables(win):
@@ -86,19 +86,16 @@
 
 
 def gather_kernel(
-    off_ref, phase_ref, absorb_ref, field_ref, corner_ref,
-    raw, made, line, raw_sem, turn_sem, line_send, line_recv, send_sem, recv_sem,
+    off_ref, raw, field_ref, corner_ref,
+    near_off, made, line, off_sem, turn_sem, line_send, line_recv, send_sem, recv_sem,
 ):
     scan, z, lane = place()
     groups = lax.axis_size("scan")
     planes = lax.axis_size("depth") // LANES
     rows = made.shape[1]
     rounds = planes // 4
-    loads = []
-    for part, ref in enumerate((phase_ref, absorb_ref)):
-        src = ref.at[0, pl.ds(pl.multiple_of(scan * rows, 8), rows), :]
-        loads.append(pltpu.make_async_copy(src, raw.at[part], raw_sem.at[part]))
-        loads[-1].start()
+    fetch = pltpu.make_async_copy(off_ref, near_off, off_sem)
+    fetch.start()
     to = (turned(z), LANES * turned(scan) + lane)
     stays = turned(z) == scan
     near = (-2, -1, 1, 2)
@@ -119,9 +116,9 @@
 
     lax.fori_loop(1, groups, greet, 0)
     line[...] = jnp.zeros_like(line)
-    line[:, : off_ref.shape[1]] = off_ref[...]
-    for load in loads:
-        load.wait()
+    field_ref[:, groups * rows :] = jnp.zeros((2, field_ref.shape[1] - groups * rows, field_ref.shape[2]), F32)
+    fetch.wait()
+    line[:, : near_off.shape[1]] = near_off[...]
     amp = jnp.exp(-raw[1])
     made[0] = amp * jnp.cos(raw[0])
     made[1] = amp * jnp.sin(raw[0])
@@ -199,17 +196,19 @@
     lax.fori_loop(0, groups, end_tell, 0)
 
 
-def window_kernel(off_ref, field_ref, out_ref, field):
+def window_kernel(corner_ref, field_ref, out_ref, off_ref, off_sem):
     win = out_ref.shape[-1]
     obj = field_ref.shape[-1]
-    field[:, :obj] = field_ref[...]
+    fetch = pltpu.make_async_copy(corner_ref, off_ref, off_sem)
+    fetch.start()
+    fetch.wait()
 
     def one(j, carry):
         row, col = corner(off_ref, j)
         high = lax.div(row, 8)
         low = row - 8 * high
         for part in range(2):
-            rows = field[part, pl.ds(pl.multiple_of(8 * high, 8), win + 8), :]
+            rows = field_ref[part, pl.ds(pl.multiple_of(8 * high, 8), win + 8), :]
             cols = pltpu.roll(rows, lax.rem(obj - col, obj), 1)[:, :win]
             out_ref[j, part] = pltpu.roll(cols, lax.rem(win + 8 - low, win + 8), 0)[:win]
         return carry
@@ -217,10 +216,13 @@
     lax.fori_loop(0, out_ref.shape[0], one, 0)
 
 
-def field_kernel(off_ref, got_ref, out_ref, field):
+def field_kernel(corner_ref, got_ref, out_ref, off_ref, off_sem):
     win = got_ref.shape[-1]
     obj = out_ref.shape[-1]
-    field[...] = jnp.zeros_like(field)
+    fetch = pltpu.make_async_copy(corner_ref, off_ref, off_sem)
+    fetch.start()
+    out_ref[...] = jnp.zeros_like(out_ref)
+    fetch.wait()
 
     def one(j, carry):
         row, col = corner(off_ref, j)
@@ -230,16 +232,15 @@
             tall = jnp.concatenate([got_ref[j, part], jnp.zeros((8, win), F32)], axis=0)
             tall = pltpu.roll(tall, low, 0)
             wide = jnp.concatenate([tall, jnp.zeros((win + 8, obj - win), F32)], axis=1)
-            field[part, pl.ds(pl.multiple_of(8 * high, 8), win + 8), :] += pltpu.roll(wide, col, 1)
+            out_ref[part, pl.ds(pl.multiple_of(8 * high, 8), win + 8), :] += pltpu.roll(wide, col, 1)
         return carry
 
     lax.fori_loop(0, got_ref.shape[0], one, 0)
-    out_ref[...] = field[:, :obj]
 
 
 def chain_kernel(
-    sections, num_pos, tw_ref, probe_ref, meas_ref, tab_ref, got_ref,
-    trans, exits, wave, go_sem, win_send, win_recv, grad_send, grad_recv,
+    sections, num_pos, tw_ref, probe_ref, all_meas_ref, all_tab_ref, got_ref,
+    trans, exits, wave, meas_ref, tab_ref, load_sem, go_sem, win_send, win_recv, grad_send, grad_recv,
 ):
     scan, z, lane = place()
     depth = LANES * z + lane
@@ -255,6 +256,13 @@
     def owner(k):
         return turned(lax.div(k, LANES)), LANES * z + lax.rem(k, LANES)
 
+    loads = [
+        pltpu.make_async_copy(src, dst, load_sem.at[i])
+        for i, (src, dst) in enumerate(
+            ((probe_ref, wave), (all_meas_ref.at[slot], meas_ref), (all_tab_ref, tab_ref)))
+    ]
+    for load in loads:
+        load.start()
     barrier = pltpu.get_barrier_semaphore()
 
     @pl.when(active)
@@ -265,7 +273,6 @@
                 pl.semaphore_signal(barrier, inc=1, device_id=owner(k), device_id_type=MESH)
             return carry
         lax.fori_loop(0, sections, greet, 0)
-        pl.semaphore_wait(barrier, sections - 1)
 
     @pl.when(jnp.logical_not(active))
     def _():
@@ -273,6 +280,13 @@
             pl.semaphore_signal(barrier, inc=1, device_id=home(j, z), device_id_type=MESH)
             return carry
         lax.fori_loop(0, num_pos, greet, 0)
+
+    @pl.when(active)
+    def _():
+        pl.semaphore_wait(barrier, sections - 1)
+
+    @pl.when(jnp.logical_not(active))
+    def _():
         pl.semaphore_wait(barrier, num_pos)
 
     def is_here(j):
@@ -327,10 +341,11 @@
             src_ref=exits.at[k], dst_ref=got_ref.at[member], send_sem=grad_send.at[k],
             recv_sem=grad_recv.at[member], device_id=owner(k), device_id_type=MESH)
 
+    for load in loads:
+        load.wait()
+
     @pl.when(active)
     def _():
-        wave[...] = probe_ref[...]
-
         def step_in(k):
             pltpu.make_async_copy(tw_ref.at[0], trans.at[k], win_recv.at[k]).wait()
             tr, ti = trans[k, 0], trans[k, 1]
@@ -349,10 +364,10 @@
             wave[1] = wi
             return carry
 
-        lax.fori_loop(0, sections - 1, forward, 0)
+        lax.fori_loop(0, sections - 1, forward, 0, unroll=2)
         er, ei = step_in(sections - 1)
         fr, fi = sandwich(er, ei, tab_ref, 4, 6)
-        resid = fr * fr + fi * fi - meas_ref[slot]
+        resid = fr * fr + fi * fi - meas_ref[...]
         lr, li = sandwich(resid * fr, resid * fi, tab_ref, 6, 4)
         wave[0] = lr
         wave[1] = li
@@ -381,7 +396,7 @@
             wave[1] = wi
             return carry
 
-        lax.fori_loop(0, sections - 1, backward, 0)
+        lax.fori_loop(0, sections - 1, backward, 0, unroll=2)
         grads(0)
 
     def finish(j, carry):
@@ -493,25 +508,26 @@
     num_pos = offsets.shape[0]
     sections = lax.axis_size("depth")
     vmem = pl.BlockSpec(memory_space=pltpu.VMEM)
-    smem = pl.BlockSpec(memory_space=pltpu.SMEM)
     anywhere = pl.BlockSpec(memory_space=pl.ANY)
     limit = 48 * 1024 * 1024
     groups = lax.axis_size("scan")
     rows = obj // groups
     rounds = sections // LANES // 4
+    first = lax.axis_index("scan") * rows
+    raw = jnp.concatenate([lax.dynamic_slice_in_dim(values, first, rows, axis=1) for values in (phase, absorb)])
     field, corners = pl.pallas_call(
         gather_kernel,
         out_shape=[
-            jax.ShapeDtypeStruct((2, obj, obj), F32),
+            jax.ShapeDtypeStruct((2, obj + 8, obj), F32),
             jax.ShapeDtypeStruct((groups, 128), jnp.int32),
         ],
-        in_specs=[vmem, anywhere, anywhere],
+        in_specs=[anywhere, vmem],
         out_specs=[vmem, vmem],
         scratch_shapes=[
-            pltpu.VMEM((2, rows, obj), F32),
+            pltpu.VMEM((num_pos, 2), jnp.int32),
             pltpu.VMEM((2, rows, obj), F32),
             pltpu.VMEM((num_pos, 128), jnp.int32),
-            pltpu.SemaphoreType.DMA((2,)),
+            pltpu.SemaphoreType.DMA,
             pltpu.SemaphoreType.DMA((2,)),
             pltpu.SemaphoreType.DMA((groups,)),
             pltpu.SemaphoreType.DMA((groups,)),
@@ -519,25 +535,28 @@
             pltpu.SemaphoreType.DMA((2, rounds, 2)),
         ],
         compiler_params=pltpu.CompilerParams(
-            collective_id=2, has_side_effects=True, vmem_limit_bytes=60 * 1024 * 1024),
-    )(offsets, phase, absorb)
+            collective_id=2, has_side_effects=True, vmem_limit_bytes=48 * 1024 * 1024),
+    )(offsets, raw)
     windows = pl.pallas_call(
         window_kernel,
         out_shape=jax.ShapeDtypeStruct((num_pos, 2, win, win), F32),
-        in_specs=[smem, vmem],
+        in_specs=[vmem, vmem],
         out_specs=vmem,
-        scratch_shapes=[pltpu.VMEM((2, obj + 8, obj), F32)],
+        scratch_shapes=[pltpu.SMEM((groups, 128), jnp.int32), pltpu.SemaphoreType.DMA],
         compiler_params=pltpu.CompilerParams(vmem_limit_bytes=limit),
     )(corners, field)
     got = pl.pallas_call(
         functools.partial(chain_kernel, sections, num_pos),
         out_shape=jax.ShapeDtypeStruct((num_pos, 2, win, win), F32),
-        in_specs=[vmem] * 4,
+        in_specs=[vmem, anywhere, anywhere, anywhere],
         out_specs=vmem,
         scratch_shapes=[
             pltpu.VMEM((sections, 2, win, win), F32),
             pltpu.VMEM((sections, 2, win, win), F32),
             pltpu.VMEM((2, win, win), F32),
+            pltpu.VMEM((win, win), F32),
+            pltpu.VMEM(tab.shape, BF16),
+            pltpu.SemaphoreType.DMA((3,)),
             pltpu.SemaphoreType.REGULAR,
             pltpu.SemaphoreType.DMA((num_pos,)),
             pltpu.SemaphoreType.DMA((sections,)),
@@ -549,10 +568,10 @@
     )(windows, probe, measured, tab)
     fields = pl.pallas_call(
         field_kernel,
-        out_shape=jax.ShapeDtypeStruct((2, obj, obj), F32),
-        in_specs=[smem, vmem],
+        out_shape=jax.ShapeDtypeStruct((2, obj + 8, obj), F32),
+        in_specs=[vmem, vmem],
         out_specs=vmem,
-        scratch_shapes=[pltpu.VMEM((2, obj + 8, obj), F32)],
+        scratch_shapes=[pltpu.SMEM((groups, 128), jnp.int32), pltpu.SemaphoreType.DMA],
         compiler_params=pltpu.CompilerParams(vmem_limit_bytes=limit),
     )(corners, got)
     return pl.pallas_call(

time: 168 us -> 161 us (0.958)
  the two profiles are of different devices: /device:TPU:33 before, /device:TPU:3 now
where the time goes in v4:
time: 161 us
  Pallas kernels  158 us (98%)
  local copies, waits for them, and re-layouts  2.8 us (2%)
    pallas_call x1, Pallas kernels, shards(): pl.pallas_call(functools.partial(chain_kernel, sections, num_pos), out_sh...  55.8 us
    pallas_call x1, Pallas kernels, shards(): pl.pallas_call(sum_kernel, out_shape=[jax.ShapeDtypeStruct((1, rows, obj)...  53.9 us
    pallas_call x1, Pallas kernels, shards(): pl.pallas_call(gather_kernel, out_shape=[jax.ShapeDtypeStruct((2, obj + 8...  43.5 us

profile of v4, /device:TPU:3, one launch (start us, length us, event | category | flops | bytes accessed | tf_op | source)
XLA Modules:
  0.0 161.1 jit_solution(3972412800463279260)
XLA Ops:
  0.6 0.8 copy.8.off_ref
  1.4 0.8 constant_dynamic-slice_fusion
  2.2 0.0 copy-start
  2.2 0.0 copy-start.1
  2.2 0.0 copy-start.2
  2.2 43.5 %shard_map.77 = (f32[2,392,384]{2,1,0:T(8,128)S(1)}, s32[16,128]{1,0:T(8,128)S(1)}) custom-call(s32[8,2]{1,0:T(8,128)S(1)} %copy.8.off_ref, f32[2,24,384]{2,1,0:T(8,128)S(1)} %pad_maximum_fusion.raw), custom_call_target="tpu_custom_call" | custom-call | tf_op jit(solution)/shard_map/pallas_call | solution.py:518
  45.7 2.4 %shard_map.78.tw_ref = f32[8,2,128,128]{3,2,1,0:T(8,128)S(1)} custom-call(s32[16,128]{1,0:T(8,128)S(1)} %get-tuple-element.4.corner_ref, f32[2,392,384]{2,1,0:T(8,128)S(1)} %get-tuple-element.5.field_ref), custom_call_target="tpu_custom_call" | custom-call | tf_op jit(solution)/shard_map/pallas_call | solution.py:540
  48.2 0.0 copy-done
  48.2 0.0 copy-done.1
  48.2 0.0 copy-done.2
  48.2 55.8 %shard_map.79.got_ref = f32[8,2,128,128]{3,2,1,0:T(8,128)S(1)} custom-call(f32[8,2,128,128]{3,2,1,0:T(8,128)S(1)} %shard_map.78.tw_ref, f32[2,128,128]{2,1,0:T(8,128)S(1)} %copy-done.2, f32[8,128,128]{2,1,0:T(8,128)S(1)} %copy-done.1, bf16[8,256,256]{2,1,0:T(8,128)(2,1)S(1)} %copy-done), custom_call_target="tpu_custom_call" | custom-call | tf_op jit(solution)/shard_map/pallas_call | solution.py:548
  104.0 1.9 %shard_map.80.parts_ref = f32[2,392,384]{2,1,0:T(8,128)S(1)} custom-call(s32[16,128]{1,0:T(8,128)S(1)} %get-tuple-element.4.corner_ref, f32[8,2,128,128]{3,2,1,0:T(8,128)S(1)} %shard_map.79.got_ref), custom_call_target="tpu_custom_call" | custom-call | tf_op jit(solution)/shard_map/pallas_call | solution.py:569
  106.0 53.9 %shard_map.81 = (f32[1,24,384]{2,1,0:T(8,128)S(1)}, f32[1,24,384]{2,1,0:T(8,128)S(1)}) custom-call(f32[2,392,384]{2,1,0:T(8,128)S(1)} %shard_map.80.parts_ref), custom_call_target="tpu_custom_call" | custom-call | tf_op jit(solution)/shard_map/pallas_call | solution.py:577
  159.9 0.6 copy.11
  160.5 0.6 copy.12
  (1 shorter events, 0.0 us)
Async XLA Ops:
  2.2 46.0 %copy-start = (bf16[8,256,256]{2,1,0:T(8,128)(2,1)S(1)}, bf16[8,256,256]{2,1,0:T(8,128)(2,1)}, u32[]{:S(2)}) copy-start(bf16[8,256,256]{2,1,0:T(8,128)(2,1)} %constant.14.clone.all_tab_ref) | copy-start | bytes 3145732
  2.2 46.0 %copy-start.1 = (f32[8,128,128]{2,1,0:T(8,128)S(1)}, f32[8,128,128]{2,1,0:T(8,128)}, u32[]{:S(2)}) copy-start(f32[8,128,128]{2,1,0:T(8,128)} %all_meas_ref.1) | copy-start | bytes 1572868
  2.2 46.0 %copy-start.2 = (f32[2,128,128]{2,1,0:T(8,128)S(1)}, f32[2,128,128]{2,1,0:T(8,128)}, u32[]{:S(2)}) copy-start(f32[2,128,128]{2,1,0:T(8,128)} %probe_ref.1) | copy-start | bytes 393220

commit v5 on v4

--- a/solution.py
+++ b/solution.py
@@ -14,7 +14,7 @@
 F32 = jnp.float32
 LANES = 2
 SIDE = 4
-AHEAD = 14
+AHEAD = 13
 
 
 def tables(win):
@@ -123,20 +123,26 @@
     made[0] = amp * jnp.cos(raw[0])
     made[1] = amp * jnp.sin(raw[0])
 
-    turn = pltpu.make_async_remote_copy(
-        src_ref=made, dst_ref=field_ref.at[:, strip_rows(turned(scan), rows), :],
-        send_sem=turn_sem.at[0], recv_sem=turn_sem.at[1], device_id=to, device_id_type=MESH)
-    stay = pltpu.make_async_copy(made, field_ref.at[:, strip_rows(z, rows), :], turn_sem.at[1])
+    def turn(part):
+        return pltpu.make_async_remote_copy(
+            src_ref=made.at[part], dst_ref=field_ref.at[part, strip_rows(turned(scan), rows), :],
+            send_sem=turn_sem.at[0, part], recv_sem=turn_sem.at[1, part], device_id=to, device_id_type=MESH)
+
+    def stay(part):
+        return pltpu.make_async_copy(
+            made.at[part], field_ref.at[part, strip_rows(z, rows), :], turn_sem.at[1, part])
 
     @pl.when(stays)
     def _():
         pl.semaphore_wait(barrier, len(near) + groups - 1)
-        stay.start()
+        for part in range(2):
+            stay(part).start()
 
     @pl.when(jnp.logical_not(stays))
     def _():
         pl.semaphore_wait(barrier, len(near) + groups)
-        turn.start()
+        for part in range(2):
+            turn(part).start()
 
     own_line = line.at[pl.ds(lax.div(z, 2), 1), :]
     own = pltpu.make_async_copy(own_line, corner_ref.at[pl.ds(scan, 1), :], line_recv.at[scan])
@@ -153,36 +159,40 @@
         return carry
 
     lax.fori_loop(1, groups, start_tell, 0)
-    stay.wait()
-
-    def passing(step, way, distance):
+
+    def passing(step, way, distance, part):
         sign = 1 if way == 0 else -1
         whose = lax.rem(z + planes - sign * 2 * step, planes)
-        block = field_ref.at[:, strip_rows(whose, rows), :]
+        block = field_ref.at[part, strip_rows(whose, rows), :]
         return pltpu.make_async_remote_copy(
             src_ref=block, dst_ref=block,
-            send_sem=send_sem.at[way, step, distance - 1], recv_sem=recv_sem.at[way, step, distance - 1],
+            send_sem=send_sem.at[way, step, distance - 1, part], recv_sem=recv_sem.at[way, step, distance - 1, part],
             device_id=around(scan, z, lane, planes, sign * distance), device_id_type=MESH)
 
     def goes(step, way, distance):
         return not (way == 1 and step == rounds - 1 and distance == 2)
 
-    plan = [(step, way, distance) for step in range(rounds) for distance in (2, 1) for way in range(2)
+    plan = [(step, way, distance, part)
+            for step in range(rounds) for part in range(2) for distance in (2, 1) for way in range(2)
             if goes(step, way, distance)]
-    for step, way, distance in plan:
+    for step, way, distance, part in plan:
+        if step == 0 and distance == 2 and way == 0:
+            stay(part).wait()
         if step > 0 and (distance == 2 or not goes(step, way, 2)):
-            passing(step - 1, way, 2).wait_recv()
-        passing(step, way, distance).start()
-    passing(rounds - 1, 0, 2).wait_recv()
-    for step, way, distance in plan:
+            passing(step - 1, way, 2, part).wait_recv()
+        passing(step, way, distance, part).start()
+    for part in range(2):
+        passing(rounds - 1, 0, 2, part).wait_recv()
+    for step, way, distance, part in plan:
         if distance == 1:
-            passing(step, way, distance).wait_recv()
-    for step, way, distance in plan:
-        passing(step, way, distance).wait_send()
+            passing(step, way, distance, part).wait_recv()
+    for step, way, distance, part in plan:
+        passing(step, way, distance, part).wait_send()
 
     @pl.when(jnp.logical_not(stays))
     def _():
-        turn.wait_send()
+        for part in range(2):
+            turn(part).wait_send()
 
     def end_tell(step, carry):
         one = lax.rem(scan + step, groups)
@@ -198,7 +208,6 @@
 
 def window_kernel(corner_ref, field_ref, out_ref, off_ref, off_sem):
     win = out_ref.shape[-1]
-    obj = field_ref.shape[-1]
     fetch = pltpu.make_async_copy(corner_ref, off_ref, off_sem)
     fetch.start()
     fetch.wait()
@@ -207,9 +216,12 @@
         row, col = corner(off_ref, j)
         high = lax.div(row, 8)
         low = row - 8 * high
+        side = lax.min(lax.div(col, win), 1)
+        tall = pl.ds(pl.multiple_of(8 * high, 8), win + 8)
+        wide = pl.ds(pl.multiple_of(win * side, win), 2 * win)
         for part in range(2):
-            rows = field_ref[part, pl.ds(pl.multiple_of(8 * high, 8), win + 8), :]
-            cols = pltpu.roll(rows, lax.rem(obj - col, obj), 1)[:, :win]
+            rows = field_ref[part, tall, wide]
+            cols = pltpu.roll(rows, lax.rem(2 * win - (col - win * side), 2 * win), 1)[:, :win]
             out_ref[j, part] = pltpu.roll(cols, lax.rem(win + 8 - low, win + 8), 0)[:win]
         return carry
 
@@ -218,7 +230,6 @@
 
 def field_kernel(corner_ref, got_ref, out_ref, off_ref, off_sem):
     win = got_ref.shape[-1]
-    obj = out_ref.shape[-1]
     fetch = pltpu.make_async_copy(corner_ref, off_ref, off_sem)
     fetch.start()
     out_ref[...] = jnp.zeros_like(out_ref)
@@ -228,11 +239,14 @@
         row, col = corner(off_ref, j)
         high = lax.div(row, 8)
         low = row - 8 * high
+        side = lax.min(lax.div(col, win), 1)
+        tall = pl.ds(pl.multiple_of(8 * high, 8), win + 8)
+        wide = pl.ds(pl.multiple_of(win * side, win), 2 * win)
         for part in range(2):
-            tall = jnp.concatenate([got_ref[j, part], jnp.zeros((8, win), F32)], axis=0)
-            tall = pltpu.roll(tall, low, 0)
-            wide = jnp.concatenate([tall, jnp.zeros((win + 8, obj - win), F32)], axis=1)
-            out_ref[part, pl.ds(pl.multiple_of(8 * high, 8), win + 8), :] += pltpu.roll(wide, col, 1)
+            block = jnp.concatenate([got_ref[j, part], jnp.zeros((8, win), F32)], axis=0)
+            block = pltpu.roll(block, low, 0)
+            block = jnp.concatenate([block, jnp.zeros((win + 8, win), F32)], axis=1)
+            out_ref[part, tall, wide] += pltpu.roll(block, col - win * side, 1)
         return carry
 
     lax.fori_loop(0, got_ref.shape[0], one, 0)
@@ -418,7 +432,7 @@
         lax.fori_loop(0, sections, drain, 0)
 
 
-def sum_kernel(parts_ref, phase_ref, absorb_ref, got, made, last, turn_sem, send_sem, recv_sem):
+def sum_kernel(parts_ref, both_ref, got, made, last, turn_sem, send_sem, recv_sem):
     scan, z, lane = place()
     planes = lax.axis_size("depth") // LANES
     rows = last.shape[2]
@@ -440,66 +454,80 @@
     def _():
         pl.semaphore_wait(barrier, len(near))
 
-    def strip(way, ahead):
+    def strip(way, ahead, part):
         sign = 1 if way == 0 else -1
-        return parts_ref.at[:, strip_rows(lax.rem(z + planes + sign * ahead, planes), rows), :]
+        return parts_ref.at[part, strip_rows(lax.rem(z + planes + sign * ahead, planes), rows), :]
 
     def goes(step, way, distance):
         return not (way == 1 and step == 0 and distance == 2)
 
-    def passing(step, way, distance):
+    def passing(step, way, distance, part):
         ahead = planes // 2 - 2 * step - (2 - distance)
-        bare = distance == 1 or step == 0 or (way == 1 and step == 0)
+        bare = distance == 1 or step == 0
         return pltpu.make_async_remote_copy(
-            src_ref=strip(way, ahead) if bare else made.at[way, step - 1],
-            dst_ref=got.at[way, step, distance - 1],
-            send_sem=send_sem.at[way, step, distance - 1], recv_sem=recv_sem.at[way, step, distance - 1],
+            src_ref=strip(way, ahead, part) if bare else made.at[way, step - 1, part],
+            dst_ref=got.at[way, step, distance - 1, part],
+            send_sem=send_sem.at[way, step, distance - 1, part],
+            recv_sem=recv_sem.at[way, step, distance - 1, part],
             device_id=around(scan, z, lane, planes, distance if way == 0 else -distance), device_id_type=MESH)
 
-    def arrived(step, way):
-        passing(step, way, 1).wait_recv()
-        total = got[way, step, 0]
+    def arrived(step, way, part):
+        passing(step, way, 1, part).wait_recv()
+        total = got[way, step, 0, part]
         if goes(step, way, 2):
-            passing(step, way, 2).wait_recv()
-            total = total + got[way, step, 1]
+            passing(step, way, 2, part).wait_recv()
+            total = total + got[way, step, 1, part]
         return total
 
-    for way in range(2):
-        if goes(0, way, 2):
-            passing(0, way, 2).start()
-    for way in range(2):
-        passing(0, way, 1).start()
-    for way in range(2):
-        passing(1, way, 1).start()
+    for part in range(2):
+        for way in range(2):
+            if goes(0, way, 2):
+                passing(0, way, 2, part).start()
+        for way in range(2):
+            passing(0, way, 1, part).start()
+    for part in range(2):
+        for way in range(2):
+            passing(1, way, 1, part).start()
     for step in range(1, rounds):
-        for way in range(2):
-            ahead = planes // 2 - 2 * step
-            made[way, step - 1] = strip(way, ahead)[...] + arrived(step - 1, way)
-            passing(step, way, 2).start()
-        if step + 1 < rounds:
+        for part in range(2):
             for way in range(2):
-                passing(step + 1, way, 1).start()
-    last[0] = strip(0, 0)[...] + (arrived(rounds - 1, 0) + arrived(rounds - 1, 1))
-    turn = pltpu.make_async_remote_copy(
-        src_ref=last.at[0], dst_ref=last.at[1], send_sem=turn_sem.at[0], recv_sem=turn_sem.at[1],
-        device_id=to, device_id_type=MESH)
-
-    @pl.when(jnp.logical_not(stays))
-    def _():
-        turn.start()
-        turn.wait()
-
-    @pl.when(stays)
-    def _():
-        last[1] = last[0]
-
-    phase_ref[0] = last[1, 0]
-    absorb_ref[0] = last[1, 1]
+                ahead = planes // 2 - 2 * step
+                made[way, step - 1, part] = strip(way, ahead, part)[...] + arrived(step - 1, way, part)
+                passing(step, way, 2, part).start()
+            if step + 1 < rounds:
+                for way in range(2):
+                    passing(step + 1, way, 1, part).start()
+
+    def turn(part):
+        return pltpu.make_async_remote_copy(
+            src_ref=last.at[0, part], dst_ref=last.at[1, part],
+            send_sem=turn_sem.at[0, part], recv_sem=turn_sem.at[1, part],
+            device_id=to, device_id_type=MESH)
+
+    for part in range(2):
+        total = strip(0, 0, part)[...] + (arrived(rounds - 1, 0, part) + arrived(rounds - 1, 1, part))
+        last[0, part] = total
+
+        @pl.when(jnp.logical_not(stays))
+        def _():
+            turn(part).start()
+
+    for part in range(2):
+        @pl.when(jnp.logical_not(stays))
+        def _():
+            turn(part).wait()
+            both_ref[part] = last[1, part]
+
+        @pl.when(stays)
+        def _():
+            both_ref[part] = last[0, part]
+
     for step in range(rounds):
         for way in range(2):
             for distance in (1, 2):
                 if goes(step, way, distance):
-                    passing(step, way, distance).wait_send()
+                    for part in range(2):
+                        passing(step, way, distance, part).wait_send()
 
 
 def shards(tab, phase, absorb, probe, offsets, measured):
@@ -528,11 +556,11 @@
             pltpu.VMEM((2, rows, obj), F32),
             pltpu.VMEM((num_pos, 128), jnp.int32),
             pltpu.SemaphoreType.DMA,
-            pltpu.SemaphoreType.DMA((2,)),
+            pltpu.SemaphoreType.DMA((2, 2)),
             pltpu.SemaphoreType.DMA((groups,)),
             pltpu.SemaphoreType.DMA((groups,)),
-            pltpu.SemaphoreType.DMA((2, rounds, 2)),
-            pltpu.SemaphoreType.DMA((2, rounds, 2)),
+            pltpu.SemaphoreType.DMA((2, rounds, 2, 2)),
+            pltpu.SemaphoreType.DMA((2, rounds, 2, 2)),
         ],
         compiler_params=pltpu.CompilerParams(
             collective_id=2, has_side_effects=True, vmem_limit_bytes=48 * 1024 * 1024),
@@ -574,22 +602,23 @@
         scratch_shapes=[pltpu.SMEM((groups, 128), jnp.int32), pltpu.SemaphoreType.DMA],
         compiler_params=pltpu.CompilerParams(vmem_limit_bytes=limit),
     )(corners, got)
-    return pl.pallas_call(
+    both = pl.pallas_call(
         sum_kernel,
-        out_shape=[jax.ShapeDtypeStruct((1, rows, obj), F32)] * 2,
+        out_shape=jax.ShapeDtypeStruct((2, rows, obj), F32),
         in_specs=[vmem],
-        out_specs=[vmem, vmem],
+        out_specs=vmem,
         scratch_shapes=[
             pltpu.VMEM((2, rounds, 2, 2, rows, obj), F32),
             pltpu.VMEM((2, rounds - 1, 2, rows, obj), F32),
             pltpu.VMEM((2, 2, rows, obj), F32),
-            pltpu.SemaphoreType.DMA((2,)),
-            pltpu.SemaphoreType.DMA((2, rounds, 2)),
-            pltpu.SemaphoreType.DMA((2, rounds, 2)),
+            pltpu.SemaphoreType.DMA((2, 2)),
+            pltpu.SemaphoreType.DMA((2, rounds, 2, 2)),
+            pltpu.SemaphoreType.DMA((2, rounds, 2, 2)),
         ],
         compiler_params=pltpu.CompilerParams(
             collective_id=1, has_side_effects=True, vmem_limit_bytes=limit),
     )(fields)
+    return both[:1], both[1:]
 
 
 def solution(mesh):

time: 161 us -> 157 us (0.975)
  the two profiles are of different devices: /device:TPU:3 before, /device:TPU:33 now
where the time goes in v5:
time: 157 us
  Pallas kernels  154 us (98%)
  local copies, waits for them, and re-layouts  2.2 us (1%)
    pallas_call x1, Pallas kernels, shards(): pl.pallas_call(functools.partial(chain_kernel, sections, num_pos), out_sh...  71.9 us
    pallas_call x1, Pallas kernels, shards(): pl.pallas_call(gather_kernel, out_shape=[jax.ShapeDtypeStruct((2, obj + 8...  40.9 us
    pallas_call x1, Pallas kernels, shards(): pl.pallas_call(sum_kernel, out_shape=jax.ShapeDtypeStruct((2, rows, obj),...  37.3 us

profile of v5, /device:TPU:33, one launch (start us, length us, event | category | flops | bytes accessed | tf_op | source)
XLA Modules:
  0.0 157.0 jit_solution(2656452347851885700)
XLA Ops:
  0.6 0.8 copy.8.off_ref
  1.4 0.8 constant_dynamic-slice_fusion
  2.2 0.0 copy-start
  2.2 0.0 copy-start.1
  2.2 0.0 copy-start.2
  2.2 40.9 %shard_map.77 = (f32[2,392,384]{2,1,0:T(8,128)S(1)}, s32[16,128]{1,0:T(8,128)S(1)}) custom-call(s32[8,2]{1,0:T(8,128)S(1)} %copy.8.off_ref, f32[2,24,384]{2,1,0:T(8,128)S(1)} %pad_maximum_fusion.raw), custom_call_target="tpu_custom_call" | custom-call | tf_op jit(solution)/shard_map/pallas_call | solution.py:546
  43.2 2.1 %shard_map.78.tw_ref = f32[8,2,128,128]{3,2,1,0:T(8,128)S(1)} custom-call(s32[16,128]{1,0:T(8,128)S(1)} %get-tuple-element.4.corner_ref, f32[2,392,384]{2,1,0:T(8,128)S(1)} %get-tuple-element.5.field_ref), custom_call_target="tpu_custom_call" | custom-call | tf_op jit(solution)/shard_map/pallas_call | solution.py:568
  45.2 0.0 copy-done
  45.2 0.0 copy-done.1
  45.3 0.0 copy-done.2
  45.3 71.9 %shard_map.79.got_ref = f32[8,2,128,128]{3,2,1,0:T(8,128)S(1)} custom-call(f32[8,2,128,128]{3,2,1,0:T(8,128)S(1)} %shard_map.78.tw_ref, f32[2,128,128]{2,1,0:T(8,128)S(1)} %copy-done.2, f32[8,128,128]{2,1,0:T(8,128)S(1)} %copy-done.1, bf16[8,256,256]{2,1,0:T(8,128)(2,1)S(1)} %copy-done), custom_call_target="tpu_custom_call" | custom-call | tf_op jit(solution)/shard_map/pallas_call | solution.py:576
  117.2 1.8 %shard_map.80.parts_ref = f32[2,392,384]{2,1,0:T(8,128)S(1)} custom-call(s32[16,128]{1,0:T(8,128)S(1)} %get-tuple-element.4.corner_ref, f32[8,2,128,128]{3,2,1,0:T(8,128)S(1)} %shard_map.79.got_ref), custom_call_target="tpu_custom_call" | custom-call | tf_op jit(solution)/shard_map/pallas_call | solution.py:597
  119.0 37.3 %shard_map.81 = f32[2,24,384]{2,1,0:T(8,128)S(1)} custom-call(f32[2,392,384]{2,1,0:T(8,128)S(1)} %shard_map.80.parts_ref), custom_call_target="tpu_custom_call" | custom-call | tf_op jit(solution)/shard_map/pallas_call | solution.py:605
  156.4 0.6 fusion
  (1 shorter events, 0.0 us)
Async XLA Ops:
  2.2 43.1 %copy-start = (bf16[8,256,256]{2,1,0:T(8,128)(2,1)S(1)}, bf16[8,256,256]{2,1,0:T(8,128)(2,1)}, u32[]{:S(2)}) copy-start(bf16[8,256,256]{2,1,0:T(8,128)(2,1)} %constant.14.clone.all_tab_ref) | copy-start | bytes 3145732
  2.2 43.0 %copy-start.1 = (f32[8,128,128]{2,1,0:T(8,128)S(1)}, f32[8,128,128]{2,1,0:T(8,128)}, u32[]{:S(2)}) copy-start(f32[8,128,128]{2,1,0:T(8,128)} %all_meas_ref.1) | copy-start | bytes 1572868
  2.2 43.0 %copy-start.2 = (f32[2,128,128]{2,1,0:T(8,128)S(1)}, f32[2,128,128]{2,1,0:T(8,128)}, u32[]{:S(2)}) copy-start(f32[2,128,128]{2,1,0:T(8,128)} %probe_ref.1) | copy-start | bytes 393220

commit v6 on v5

--- a/solution.py
+++ b/solution.py
@@ -169,20 +169,20 @@
             send_sem=send_sem.at[way, step, distance - 1, part], recv_sem=recv_sem.at[way, step, distance - 1, part],
             device_id=around(scan, z, lane, planes, sign * distance), device_id_type=MESH)
 
-    def goes(step, way, distance):
-        return not (way == 1 and step == rounds - 1 and distance == 2)
+    def goes(step, way, distance, part):
+        return not (way == 1 - part and step == rounds - 1 and distance == 2)
 
     plan = [(step, way, distance, part)
             for step in range(rounds) for part in range(2) for distance in (2, 1) for way in range(2)
-            if goes(step, way, distance)]
+            if goes(step, way, distance, part)]
     for step, way, distance, part in plan:
         if step == 0 and distance == 2 and way == 0:
             stay(part).wait()
-        if step > 0 and (distance == 2 or not goes(step, way, 2)):
+        if step > 0 and (distance == 2 or not goes(step, way, 2, part)):
             passing(step - 1, way, 2, part).wait_recv()
         passing(step, way, distance, part).start()
     for part in range(2):
-        passing(rounds - 1, 0, 2, part).wait_recv()
+        passing(rounds - 1, part, 2, part).wait_recv()
     for step, way, distance, part in plan:
         if distance == 1:
             passing(step, way, distance, part).wait_recv()
@@ -378,7 +378,7 @@
             wave[1] = wi
             return carry
 
-        lax.fori_loop(0, sections - 1, forward, 0, unroll=2)
+        lax.fori_loop(0, sections - 1, forward, 0, unroll=4)
         er, ei = step_in(sections - 1)
         fr, fi = sandwich(er, ei, tab_ref, 4, 6)
         resid = fr * fr + fi * fi - meas_ref[...]
@@ -410,7 +410,7 @@
             wave[1] = wi
             return carry
 
-        lax.fori_loop(0, sections - 1, backward, 0, unroll=2)
+        lax.fori_loop(0, sections - 1, backward, 0, unroll=4)
         grads(0)
 
     def finish(j, carry):
@@ -458,8 +458,8 @@
         sign = 1 if way == 0 else -1
         return parts_ref.at[part, strip_rows(lax.rem(z + planes + sign * ahead, planes), rows), :]
 
-    def goes(step, way, distance):
-        return not (way == 1 and step == 0 and distance == 2)
+    def goes(step, way, distance, part):
+        return not (way == 1 - part and step == 0 and distance == 2)
 
     def passing(step, way, distance, part):
         ahead = planes // 2 - 2 * step - (2 - distance)
@@ -474,14 +474,14 @@
     def arrived(step, way, part):
         passing(step, way, 1, part).wait_recv()
         total = got[way, step, 0, part]
-        if goes(step, way, 2):
+        if goes(step, way, 2, part):
             passing(step, way, 2, part).wait_recv()
             total = total + got[way, step, 1, part]
         return total
 
     for part in range(2):
         for way in range(2):
-            if goes(0, way, 2):
+            if goes(0, way, 2, part):
                 passing(0, way, 2, part).start()
         for way in range(2):
             passing(0, way, 1, part).start()
@@ -525,8 +525,8 @@
     for step in range(rounds):
         for way in range(2):
             for distance in (1, 2):
-                if goes(step, way, distance):
-                    for part in range(2):
+                for part in range(2):
+                    if goes(step, way, distance, part):
                         passing(step, way, distance, part).wait_send()
 
 

time: 157 us -> 156 us (level)
  no operation moved by 1% of the time
where the time goes in v6:
time: 156 us
  Pallas kernels  153 us (98%)
  local copies, waits for them, and re-layouts  2.2 us (1%)
    pallas_call x1, Pallas kernels, shards(): pl.pallas_call(functools.partial(chain_kernel, sections, num_pos), out_sh...  72.7 us
    pallas_call x1, Pallas kernels, shards(): pl.pallas_call(gather_kernel, out_shape=[jax.ShapeDtypeStruct((2, obj + 8...  39.8 us
    pallas_call x1, Pallas kernels, shards(): pl.pallas_call(sum_kernel, out_shape=jax.ShapeDtypeStruct((2, rows, obj),...  36.6 us

profile of v6, /device:TPU:33, one launch (start us, length us, event | category | flops | bytes accessed | tf_op | source)
XLA Modules:
  0.0 155.9 jit_solution(12184679900991098443)
XLA Ops:
  0.6 0.8 copy.8.off_ref
  1.4 0.8 constant_dynamic-slice_fusion
  2.2 0.0 copy-start
  2.2 0.0 copy-start.1
  2.2 0.0 copy-start.2
  2.2 39.8 %shard_map.77 = (f32[2,392,384]{2,1,0:T(8,128)S(1)}, s32[16,128]{1,0:T(8,128)S(1)}) custom-call(s32[8,2]{1,0:T(8,128)S(1)} %copy.8.off_ref, f32[2,24,384]{2,1,0:T(8,128)S(1)} %pad_maximum_fusion.raw), custom_call_target="tpu_custom_call" | custom-call | tf_op jit(solution)/shard_map/pallas_call | solution.py:546
  42.0 2.1 %shard_map.78.tw_ref = f32[8,2,128,128]{3,2,1,0:T(8,128)S(1)} custom-call(s32[16,128]{1,0:T(8,128)S(1)} %get-tuple-element.4.corner_ref, f32[2,392,384]{2,1,0:T(8,128)S(1)} %get-tuple-element.5.field_ref), custom_call_target="tpu_custom_call" | custom-call | tf_op jit(solution)/shard_map/pallas_call | solution.py:568
  44.1 0.0 copy-done
  44.1 0.0 copy-done.1
  44.1 0.0 copy-done.2
  44.1 72.7 %shard_map.79.got_ref = f32[8,2,128,128]{3,2,1,0:T(8,128)S(1)} custom-call(f32[8,2,128,128]{3,2,1,0:T(8,128)S(1)} %shard_map.78.tw_ref, f32[2,128,128]{2,1,0:T(8,128)S(1)} %copy-done.2, f32[8,128,128]{2,1,0:T(8,128)S(1)} %copy-done.1, bf16[8,256,256]{2,1,0:T(8,128)(2,1)S(1)} %copy-done), custom_call_target="tpu_custom_call" | custom-call | tf_op jit(solution)/shard_map/pallas_call | solution.py:576
  116.8 1.8 %shard_map.80.parts_ref = f32[2,392,384]{2,1,0:T(8,128)S(1)} custom-call(s32[16,128]{1,0:T(8,128)S(1)} %get-tuple-element.4.corner_ref, f32[8,2,128,128]{3,2,1,0:T(8,128)S(1)} %shard_map.79.got_ref), custom_call_target="tpu_custom_call" | custom-call | tf_op jit(solution)/shard_map/pallas_call | solution.py:597
  118.7 36.6 %shard_map.81 = f32[2,24,384]{2,1,0:T(8,128)S(1)} custom-call(f32[2,392,384]{2,1,0:T(8,128)S(1)} %shard_map.80.parts_ref), custom_call_target="tpu_custom_call" | custom-call | tf_op jit(solution)/shard_map/pallas_call | solution.py:605
  155.3 0.6 fusion
  (1 shorter events, 0.0 us)
Async XLA Ops:
  2.2 41.9 %copy-start = (bf16[8,256,256]{2,1,0:T(8,128)(2,1)S(1)}, bf16[8,256,256]{2,1,0:T(8,128)(2,1)}, u32[]{:S(2)}) copy-start(bf16[8,256,256]{2,1,0:T(8,128)(2,1)} %constant.14.clone.all_tab_ref) | copy-start | bytes 3145732
  2.2 41.9 %copy-start.1 = (f32[8,128,128]{2,1,0:T(8,128)S(1)}, f32[8,128,128]{2,1,0:T(8,128)}, u32[]{:S(2)}) copy-start(f32[8,128,128]{2,1,0:T(8,128)} %all_meas_ref.1) | copy-start | bytes 1572868
  2.2 41.9 %copy-start.2 = (f32[2,128,128]{2,1,0:T(8,128)S(1)}, f32[2,128,128]{2,1,0:T(8,128)}, u32[]{:S(2)}) copy-start(f32[2,128,128]{2,1,0:T(8,128)} %probe_ref.1) | copy-start | bytes 393220

commit v7 on v6

--- a/solution.py
+++ b/solution.py
@@ -378,7 +378,7 @@
             wave[1] = wi
             return carry
 
-        lax.fori_loop(0, sections - 1, forward, 0, unroll=4)
+        lax.fori_loop(0, sections - 1, forward, 0, unroll=8)
         er, ei = step_in(sections - 1)
         fr, fi = sandwich(er, ei, tab_ref, 4, 6)
         resid = fr * fr + fi * fi - meas_ref[...]
@@ -410,7 +410,7 @@
             wave[1] = wi
             return carry
 
-        lax.fori_loop(0, sections - 1, backward, 0, unroll=4)
+        lax.fori_loop(0, sections - 1, backward, 0, unroll=8)
         grads(0)
 
     def finish(j, carry):

time: 156 us -> 157 us (level)
  the two profiles are of different devices: /device:TPU:33 before, /device:TPU:199 now
where the time goes in v7:
time: 157 us; the launch traced here: 156 us
  Pallas kernels  154 us (98%)
  local copies, waits for them, and re-layouts  2.2 us (1%)
    pallas_call x1, Pallas kernels, shards(): pl.pallas_call(functools.partial(chain_kernel, sections, num_pos), out_sh...  57.8 us
    pallas_call x1, Pallas kernels, shards(): pl.pallas_call(sum_kernel, out_shape=jax.ShapeDtypeStruct((2, rows, obj),...  57.8 us
    pallas_call x1, Pallas kernels, shards(): pl.pallas_call(gather_kernel, out_shape=[jax.ShapeDtypeStruct((2, obj + 8...  34.1 us

profile of v7, /device:TPU:199, one launch (start us, length us, event | category | flops | bytes accessed | tf_op | source)
XLA Modules:
  0.0 156.4 jit_solution(7499953156437083952)
XLA Ops:
  0.6 0.8 copy.8.off_ref
  1.4 0.8 constant_dynamic-slice_fusion
  2.2 0.0 copy-start
  2.2 0.0 copy-start.1
  2.2 0.0 copy-start.2
  2.2 34.1 %shard_map.77 = (f32[2,392,384]{2,1,0:T(8,128)S(1)}, s32[16,128]{1,0:T(8,128)S(1)}) custom-call(s32[8,2]{1,0:T(8,128)S(1)} %copy.8.off_ref, f32[2,24,384]{2,1,0:T(8,128)S(1)} %pad_maximum_fusion.raw), custom_call_target="tpu_custom_call" | custom-call | tf_op jit(solution)/shard_map/pallas_call | solution.py:546
  36.3 2.1 %shard_map.78.tw_ref = f32[8,2,128,128]{3,2,1,0:T(8,128)S(1)} custom-call(s32[16,128]{1,0:T(8,128)S(1)} %get-tuple-element.4.corner_ref, f32[2,392,384]{2,1,0:T(8,128)S(1)} %get-tuple-element.5.field_ref), custom_call_target="tpu_custom_call" | custom-call | tf_op jit(solution)/shard_map/pallas_call | solution.py:568
  38.4 0.0 copy-done
  38.4 0.0 copy-done.1
  38.4 0.0 copy-done.2
  38.4 57.8 %shard_map.79.got_ref = f32[8,2,128,128]{3,2,1,0:T(8,128)S(1)} custom-call(f32[8,2,128,128]{3,2,1,0:T(8,128)S(1)} %shard_map.78.tw_ref, f32[2,128,128]{2,1,0:T(8,128)S(1)} %copy-done.2, f32[8,128,128]{2,1,0:T(8,128)S(1)} %copy-done.1, bf16[8,256,256]{2,1,0:T(8,128)(2,1)S(1)} %copy-done), custom_call_target="tpu_custom_call" | custom-call | tf_op jit(solution)/shard_map/pallas_call | solution.py:576
  96.2 1.8 %shard_map.80.parts_ref = f32[2,392,384]{2,1,0:T(8,128)S(1)} custom-call(s32[16,128]{1,0:T(8,128)S(1)} %get-tuple-element.4.corner_ref, f32[8,2,128,128]{3,2,1,0:T(8,128)S(1)} %shard_map.79.got_ref), custom_call_target="tpu_custom_call" | custom-call | tf_op jit(solution)/shard_map/pallas_call | solution.py:597
  98.0 57.8 %shard_map.81 = f32[2,24,384]{2,1,0:T(8,128)S(1)} custom-call(f32[2,392,384]{2,1,0:T(8,128)S(1)} %shard_map.80.parts_ref), custom_call_target="tpu_custom_call" | custom-call | tf_op jit(solution)/shard_map/pallas_call | solution.py:605
  155.8 0.6 fusion
  (1 shorter events, 0.0 us)
Async XLA Ops:
  2.2 36.2 %copy-start = (bf16[8,256,256]{2,1,0:T(8,128)(2,1)S(1)}, bf16[8,256,256]{2,1,0:T(8,128)(2,1)}, u32[]{:S(2)}) copy-start(bf16[8,256,256]{2,1,0:T(8,128)(2,1)} %constant.14.clone.all_tab_ref) | copy-start | bytes 3145732
  2.2 36.2 %copy-start.1 = (f32[8,128,128]{2,1,0:T(8,128)S(1)}, f32[8,128,128]{2,1,0:T(8,128)}, u32[]{:S(2)}) copy-start(f32[8,128,128]{2,1,0:T(8,128)} %all_meas_ref.1) | copy-start | bytes 1572868
  2.2 36.2 %copy-start.2 = (f32[2,128,128]{2,1,0:T(8,128)S(1)}, f32[2,128,128]{2,1,0:T(8,128)}, u32[]{:S(2)}) copy-start(f32[2,128,128]{2,1,0:T(8,128)} %probe_ref.1) | copy-start | bytes 393220

commit v8 on v6

--- a/solution.py
+++ b/solution.py
@@ -14,7 +14,7 @@
 F32 = jnp.float32
 LANES = 2
 SIDE = 4
-AHEAD = 13
+AHEAD = 12
 
 
 def tables(win):

time: 156 us -> 158 us (1.013)
  the two profiles are of different devices: /device:TPU:33 before, /device:TPU:199 now
where the time goes in v8:
time: 158 us; the launch traced here: 157 us
  Pallas kernels  154 us (97%)
  local copies, waits for them, and re-layouts  2.2 us (1%)
    pallas_call x1, Pallas kernels, shards(): pl.pallas_call(functools.partial(chain_kernel, sections, num_pos), out_sh...  58.9 us
    pallas_call x1, Pallas kernels, shards(): pl.pallas_call(sum_kernel, out_shape=jax.ShapeDtypeStruct((2, rows, obj),...  57.6 us
    pallas_call x1, Pallas kernels, shards(): pl.pallas_call(gather_kernel, out_shape=[jax.ShapeDtypeStruct((2, obj + 8...  34.1 us

profile of v8, /device:TPU:199, one launch (start us, length us, event | category | flops | bytes accessed | tf_op | source)
XLA Modules:
  0.0 157.3 jit_solution(1594368124913523397)
XLA Ops:
  0.6 0.8 copy.8.off_ref
  1.4 0.8 constant_dynamic-slice_fusion
  2.2 0.0 copy-start
  2.2 0.0 copy-start.1
  2.2 0.0 copy-start.2
  2.2 34.1 %shard_map.77 = (f32[2,392,384]{2,1,0:T(8,128)S(1)}, s32[16,128]{1,0:T(8,128)S(1)}) custom-call(s32[8,2]{1,0:T(8,128)S(1)} %copy.8.off_ref, f32[2,24,384]{2,1,0:T(8,128)S(1)} %pad_maximum_fusion.raw), custom_call_target="tpu_custom_call" | custom-call | tf_op jit(solution)/shard_map/pallas_call | solution.py:546
  36.3 2.1 %shard_map.78.tw_ref = f32[8,2,128,128]{3,2,1,0:T(8,128)S(1)} custom-call(s32[16,128]{1,0:T(8,128)S(1)} %get-tuple-element.4.corner_ref, f32[2,392,384]{2,1,0:T(8,128)S(1)} %get-tuple-element.5.field_ref), custom_call_target="tpu_custom_call" | custom-call | tf_op jit(solution)/shard_map/pallas_call | solution.py:568
  38.4 0.0 copy-done
  38.4 0.0 copy-done.1
  38.4 0.0 copy-done.2
  38.4 58.9 %shard_map.79.got_ref = f32[8,2,128,128]{3,2,1,0:T(8,128)S(1)} custom-call(f32[8,2,128,128]{3,2,1,0:T(8,128)S(1)} %shard_map.78.tw_ref, f32[2,128,128]{2,1,0:T(8,128)S(1)} %copy-done.2, f32[8,128,128]{2,1,0:T(8,128)S(1)} %copy-done.1, bf16[8,256,256]{2,1,0:T(8,128)(2,1)S(1)} %copy-done), custom_call_target="tpu_custom_call" | custom-call | tf_op jit(solution)/shard_map/pallas_call | solution.py:576
  97.3 1.8 %shard_map.80.parts_ref = f32[2,392,384]{2,1,0:T(8,128)S(1)} custom-call(s32[16,128]{1,0:T(8,128)S(1)} %get-tuple-element.4.corner_ref, f32[8,2,128,128]{3,2,1,0:T(8,128)S(1)} %shard_map.79.got_ref), custom_call_target="tpu_custom_call" | custom-call | tf_op jit(solution)/shard_map/pallas_call | solution.py:597
  99.1 57.6 %shard_map.81 = f32[2,24,384]{2,1,0:T(8,128)S(1)} custom-call(f32[2,392,384]{2,1,0:T(8,128)S(1)} %shard_map.80.parts_ref), custom_call_target="tpu_custom_call" | custom-call | tf_op jit(solution)/shard_map/pallas_call | solution.py:605
  156.7 0.6 fusion
  (1 shorter events, 0.0 us)
Async XLA Ops:
  2.2 36.2 %copy-start = (bf16[8,256,256]{2,1,0:T(8,128)(2,1)S(1)}, bf16[8,256,256]{2,1,0:T(8,128)(2,1)}, u32[]{:S(2)}) copy-start(bf16[8,256,256]{2,1,0:T(8,128)(2,1)} %constant.14.clone.all_tab_ref) | copy-start | bytes 3145732
  2.2 36.2 %copy-start.1 = (f32[8,128,128]{2,1,0:T(8,128)S(1)}, f32[8,128,128]{2,1,0:T(8,128)}, u32[]{:S(2)}) copy-start(f32[8,128,128]{2,1,0:T(8,128)} %all_meas_ref.1) | copy-start | bytes 1572868
  2.2 36.2 %copy-start.2 = (f32[2,128,128]{2,1,0:T(8,128)S(1)}, f32[2,128,128]{2,1,0:T(8,128)}, u32[]{:S(2)}) copy-start(f32[2,128,128]{2,1,0:T(8,128)} %probe_ref.1) | copy-start | bytes 393220
